TPU v7x, 256 devices: a whole 4x4x8 slice. The times are simulated.
256 devices in a mesh: dp: 4 (over x), vocab: 64 (over y, z, core).
Axes of the slice: x: 4, y: 4, z: 8, core: 2. Of those that a mesh axis runs over, the one named last changes fastest.
Arguments:
- student_hidden: bfloat16 [2048, 2560], P(('dp', 'vocab')), parts along dimension 0, may hold values from -48.620019 to 48.620019
- teacher_hidden: bfloat16 [2048, 2048], P(('dp', 'vocab')), parts along dimension 0, may hold values from -54.358834 to 54.358834
- student_head: bfloat16 [10240, 81920], P('dp', 'vocab'), parts along dimension 0, may hold values from -0.118585412 to 0.118585412
- teacher_head: bfloat16 [8192, 81920], P('dp', 'vocab'), parts along dimension 0, may hold values from -0.13258252 to 0.13258252
- segment_ids: int32 [2048], P('dp'), parts along dimension 0, may hold values from 0 to 15, as said below
- valid_mask: int32 [2048], P('dp'), parts along dimension 0, may hold values from 0 to 1
Outputs:
- token_kl: float32 [2048], P(('dp', 'vocab')), parts along dimension 0
- hidden_grad: bfloat16 [2048, 2560], P(('dp', 'vocab')), parts along dimension 0
There are 4 independent parts, one for each index of `dp`. A program takes and returns all parts, laid end to end along the dimension named above; each array names one. Nothing has to cross between parts.
Inputs may be any that keep to these rules, and one draw needn't show every extreme that they name: `segment_ids`: ids never fall; each packed sequence holds 16 to 48 tokens, one exactly 48.
All inputs are finite; a program needn't handle non-finite values.
Results may differ from a plain program's by a relative error of at most 0.005.
Values may be sent and summed in bfloat16 or wider, within the bound.
A program may use at most 64 MiB of HBM per device.

v0:
```python
import jax
import jax.numpy as jnp
from jax import lax
from jax.sharding import PartitionSpec as P

SEGS = 16


LOSS_SCALE = 1024.0


def local(student_hidden, teacher_hidden, student_head, teacher_head, segment_ids, valid_mask):
    rows_dev = student_hidden.shape[0]
    part_student = jnp.dot(
        lax.all_gather(student_hidden, "vocab", axis=0, tiled=True),
        student_head,
        preferred_element_type=jnp.float32,
    )
    part_teacher = jnp.dot(
        lax.all_gather(teacher_hidden, "vocab", axis=0, tiled=True),
        teacher_head,
        preferred_element_type=jnp.float32,
    )
    log_ratio = part_student - part_teacher
    peak_student, peak_teacher = lax.pmax(
        (jnp.max(part_student, axis=1), jnp.max(part_teacher, axis=1)), "vocab"
    )
    student_exp = jnp.exp(part_student - peak_student[:, None])
    teacher_exp = jnp.exp(part_teacher - peak_teacher[:, None])
    sum_student, sum_teacher, cross = lax.psum(
        (
            jnp.sum(student_exp, axis=1),
            jnp.sum(teacher_exp, axis=1),
            jnp.sum(student_exp * log_ratio, axis=1),
        ),
        "vocab",
    )
    lse_student = peak_student + jnp.log(sum_student)
    lse_teacher = peak_teacher + jnp.log(sum_teacher)
    kl_all = cross / sum_student - lse_student + lse_teacher
    member = (segment_ids[:, None] == jnp.arange(SEGS, dtype=jnp.int32)[None, :]).astype(
        jnp.float32
    )
    valid = valid_mask.astype(jnp.float32)
    counts = jnp.sum(member * valid[:, None], axis=0)
    row_count = jnp.sum(member * counts[None, :], axis=1)
    weight = LOSS_SCALE * valid / jnp.maximum(row_count, 1.0)
    offset = lse_student - lse_teacher + kl_all
    grad_logits = (
        weight[:, None]
        * jnp.exp(part_student - lse_student[:, None])
        * (log_ratio - offset[:, None])
    ).astype(jnp.bfloat16)
    own_start = lax.axis_index("vocab") * rows_dev
    token_kl = lax.dynamic_slice_in_dim(kl_all, own_start, rows_dev, 0)
    hidden_grad = lax.psum_scatter(
        lax.dot_general(
            grad_logits, student_head, (((1,), (1,)), ((), ())), preferred_element_type=jnp.float32
        ),
        "vocab",
        scatter_dimension=0,
        tiled=True,
    ).astype(jnp.bfloat16)
    return (token_kl, hidden_grad)


def solution(mesh):
    in_specs = (
        P(("dp", "vocab"), None),
        P(("dp", "vocab"), None),
        P("dp", "vocab"),
        P("dp", "vocab"),
        P("dp"),
        P("dp"),
    )
    out_specs = (P(("dp", "vocab")), P(("dp", "vocab"), None))
    return jax.shard_map(local, mesh=mesh, in_specs=in_specs, out_specs=out_specs, check_vma=False)
```

profile of v0, /device:TPU:37, one launch (start us, length us, event | category | flops | bytes accessed | tf_op | source)
XLA Modules:
  0.0 584.5 jit_solution(14171446705578872933)
XLA Ops:
  7.2 0.0 all-gather.5.cloned.1.call-start
  7.2 0.7 all-gather.5.cloned.1.call-update
  7.9 0.0 all-gather.3.cloned.1.call-start
  7.9 0.7 all-gather.3.cloned.1.call-update
  8.6 0.0 reduce-scatter.2.cloned.1.call-start
  8.7 0.7 convert_element_type.10
  9.4 0.8 select_reduce_fusion.1
  10.2 0.8 select_reduce_fusion
  11.0 0.7 maximum_divide_fusion
  11.6 78.5 %all-gather.5.cloned.1.call-done = bf16[512,2048]{1,0:T(8,128)(2,1)} async-done(((bf16[8,2048]{1,0:T(8,128)(2,1)}), bf16[512,2048]{1,0:T(8,128)(2,1)}) %all-gather.5.cloned.1.call-update) | async-done | bytes 2097168 | tf_op jit(solution)/shard_map/all_gather | solution.py:20
  90.2 7.6 %fusion.6 = (f32[512]{0:T(512)S(1)}, f32[512,1280]{1,0:T(8,128)}) fusion(bf16[512,2048]{1,0:T(8,128)(2,1)} %all-gather.5.cloned.1.call-done, bf16[2048,1280]{1,0:T(8,128)(2,1)} %param.9), kind=kOutput, calls=%fused_computation.18 | convolution fusion | flops 2685009408 | bytes 9963520 | tf_op jit(solution)/shard_map/dot_general | solution.py:19
  97.7 70.7 %all-gather.3.cloned.1.call-done = bf16[512,2560]{1,0:T(8,128)(2,1)} async-done(((bf16[8,2560]{1,0:T(8,128)(2,1)}), bf16[512,2560]{1,0:T(8,128)(2,1)}) %all-gather.3.cloned.1.call-update) | async-done | bytes 2621456 | tf_op jit(solution)/shard_map/all_gather | solution.py:15
  168.4 7.3 %fusion.5 = (f32[512]{0:T(512)S(1)}, f32[512,1280]{1,0:T(8,128)S(1)}) fusion(bf16[512,2560]{1,0:T(8,128)(2,1)} %all-gather.3.cloned.1.call-done, bf16[2560,1280]{1,0:T(8,128)(2,1)} %param.8), kind=kOutput, calls=%fused_computation.17 | convolution fusion | flops 3356098048 | bytes 11798528 | tf_op jit(solution)/shard_map/dot_general | solution.py:14
  175.7 119.5 %all-reduce.1 = (f32[512]{0:T(512)S(1)}, f32[512]{0:T(512)S(1)}) all-reduce(f32[512]{0:T(512)S(1)} %get-tuple-element.14, f32[512]{0:T(512)S(1)} %get-tuple-element.16), channel_id=1, replica_groups=mesh['dp'=4,'vocab'=64] {'vocab'}, use_global_device_ids=true, to_apply=%region_1.0 | all-reduce | flops 1024 | bytes 8192 | tf_op jit(solution)/shard_map/pmax | solution.py:25
  295.3 4.1 multiply_reduce_fusion
  299.4 128.4 %all-reduce = (f32[512]{0:T(512)S(1)}, f32[512]{0:T(512)S(1)}, f32[512]{0:T(512)S(1)}) all-reduce(f32[512]{0:T(512)S(1)} %get-tuple-element.3, f32[512]{0:T(512)S(1)} %get-tuple-element.2, f32[512]{0:T(512)S(1)} %get-tuple-element.13), channel_id=1, replica_groups=mesh['dp'=4,'vocab'=64] {'vocab'}, use_global_device_ids=true, to_apply=%region_5.0 | all-reduce | flops 1536 | bytes 12288 | tf_op jit(solution)/shard_map/psum | solution.py:30
  427.9 9.9 %fusion.1 = f32[512,2560]{1,0:T(8,128)} fusion(bf16[2560,1280]{1,0:T(8,128)(2,1)} %param.8, f32[512,1280]{1,0:T(8,128)} %get-tuple-element.12, f32[512,1280]{1,0:T(8,128)S(1)} %get-tuple-element.15, f32[512]{0:T(512)S(1)} %get-tuple-element.9, f32[512]{0:T(512)S(1)} %get-tuple-element.11, f32[512]{0:T(512)S(1)} %maximum_divide_fusion), kind=kOutput, calls=%fused_computation.5 | convolution fusion | flops 3358720000 | bytes 17045504 | tf_op jit(solution)/shard_map/dot_general | solution.py:57
  437.7 0.0 reduce-scatter.2.cloned.1.call-update
  437.8 0.6 dynamic_slice.3
  438.3 138.1 %reduce-scatter.2.cloned.1.call-done = f32[8,2560]{1,0:T(8,128)} async-done(((f32[512,2560]{1,0:T(8,128)}), f32[8,2560]{1,0:T(8,128)}) %reduce-scatter.2.cloned.1.call-update) | async-done | bytes 81936 | tf_op jit(solution)/shard_map/reduce_scatter | solution.py:56
  576.4 1.5 convert_element_type.12
  (1 shorter events, 0.0 us)
Async XLA Ops:
  7.2 83.0 %all-gather.5.cloned.1.call-start = ((), (), s32[]{:S(2)}) async-start(), calls=%async_computation.2 | async-start | bytes 2129920 | tf_op jit(solution)/shard_map/all_gather | solution.py:20
  7.9 160.5 %all-gather.3.cloned.1.call-start = ((), (), s32[]{:S(2)}) async-start(), calls=%async_computation.1 | async-start | bytes 2662400 | tf_op jit(solution)/shard_map/all_gather | solution.py:15
  8.6 567.8 %reduce-scatter.2.cloned.1.call-start = ((), (), s32[]{:S(2)}) async-start(), calls=%async_computation.3 | async-start | bytes 5324800 | tf_op jit(solution)/shard_map/reduce_scatter | solution.py:56
Sparse Core Ops, SparseCore 0:
  10.8 79.3 all-gather.4
  92.9 75.4 all-gather.2
  437.9 138.4 reduce-scatter.1
where the time goes:
time: 591 us; the launch traced here: 584 us
  waiting for transfers between devices  289 us (49%)
  blocking collectives  248 us (42%)
  matrix products  24.8 us (4%)
  between operations  13.8 us (2%)
  other arithmetic  8.6 us (1%)
    reduce_scatter x1, waiting for transfers between devices, local(): lax.psum_scatter(lax.dot_general(grad_logits, student_head, (((1,), (1,))...  138 us
    psum x1, blocking collectives, local(): lax.psum((jnp.sum(student_exp, axis=1), jnp.sum(teacher_exp, axis=1), jnp...  128 us
    pmax x1, blocking collectives, local(): lax.pmax((jnp.max(part_student, axis=1), jnp.max(part_teacher, axis=1)),...  120 us
    all_gather x1, waiting for transfers between devices, local(): lax.all_gather(teacher_hidden, 'vocab', axis=0, tiled=True)  78.5 us
    all_gather x1, waiting for transfers between devices, local(): lax.all_gather(student_hidden, 'vocab', axis=0, tiled=True)  70.7 us
  transfers between devices with their start and end apart: 3, of which 3 were waited for; matrix products, arithmetic and copies ran while one was open for 2% of the time, Pallas kernels for 0%

commit v1 on v0

v1 whole, which is shorter than its diff:
```python
import functools

import jax
import jax.numpy as jnp
from jax import lax
from jax.experimental import pallas as pl
from jax.experimental.pallas import tpu as pltpu
from jax.sharding import PartitionSpec as P

LOSS_SCALE = 1024.0
NY, NZ, NC = 4, 8, 2
HZ = NZ // 2
BLK = 16
HALF = NY * HZ * BLK
TILE = 256
MESH = pl.DeviceIdType.MESH


def kernel(
    hs, ht, vs,
    sh_ref, th_ref, seg_ref, valid_ref, ws_hbm, wt_hbm,
    kl_ref, out_ref,
    ws, wt, x, xf, xg, logit_s, logit_t,
    stat_col, stat_own, stat_z, stat_mid, stat_y, fac, wcol,
    ps, pr, r1, ra, r2a, ra2, rb, r2b, rb2, fin, fin_in,
    load_sem, pair_s, pair_r,
    a1_s, a1_r, a2_s, a2_r, b1_s, b1_r, b2_s, b2_r, sib_s, sib_r,
    sz_s, sz_r, sy_s, sy_r, ps_s, ps_r,
    ra1_s, ra1_r, ra2_s, ra2_r, rb1_s, rb1_r, rb2_s, rb2_r, fin_s, fin_r,
):
    v = lax.axis_index("vocab")
    y, z, c = v // (NZ * NC), (v // NC) % NZ, v % NC
    zz, par = z // 2, z % 2
    hs2, ht2 = hs // 2, ht // 2
    sa, ta = (hs2 * 4 // 5) // 128 * 128, (ht2 * 3 // 4) // 128 * 128
    widths = ((sa, hs2 - sa), (ta, ht2 - ta))

    def dev(dy, dz, dc):
        return {"vocab": (((y + dy) % NY) * NZ + (z + dz) % NZ) * NC + (c + dc) % NC}

    def rcopy(src, dst, ssem, rsem, device):
        return pltpu.make_async_remote_copy(
            src_ref=src, dst_ref=dst, send_sem=ssem, recv_sem=rsem,
            device_id=device, device_id_type=MESH,
        )

    load_s = pltpu.make_async_copy(ws_hbm, ws, load_sem.at[0])
    load_t = pltpu.make_async_copy(wt_hbm, wt, load_sem.at[1])
    load_s.start()
    load_t.start()

    barrier = pltpu.get_barrier_semaphore()
    partners = [(0, k, 0) for k in range(1, NZ)]
    partners += [(j, 0, d) for j in range(1, NY) for d in range(NC)] + [(0, 0, 1)]
    for p in partners:
        pl.semaphore_signal(barrier, inc=1, device_id=dev(*p), device_id_type=MESH)
    xf[:, :hs2] = sh_ref[:, pl.ds(pl.multiple_of((1 - c) * hs2, 128), hs2)].astype(jnp.float32)
    xf[:, hs2:] = th_ref[:, pl.ds(pl.multiple_of((1 - c) * ht2, 128), ht2)].astype(jnp.float32)
    pl.semaphore_wait(barrier, len(partners))
    pair = rcopy(xf, xg, pair_s, pair_r, dev(0, 0, 1))
    pair.start()

    seg = jnp.broadcast_to(seg_ref[...].astype(jnp.float32), (128, 2 * HALF))
    val = jnp.broadcast_to(valid_ref[...].astype(jnp.float32), (128, 2 * HALF))
    seg_c, val_c = jnp.transpose(seg)[:, :1], jnp.transpose(val)[:, :1]
    same = jnp.where(seg_c == seg[:1, :], val[:1, :], 0.0)
    count = jnp.sum(same, axis=1, keepdims=True)
    weight = LOSS_SCALE * val_c / jnp.maximum(count, 1.0)
    wcol[...] = jnp.broadcast_to(weight, (2 * HALF, 128)).reshape(NY, HZ, 2, BLK, 128)

    pair.wait()

    def put(col, width, full, part):
        mine = full[:, pl.ds(pl.multiple_of(c * width, 128), width)].astype(jnp.float32)
        both = jnp.concatenate(
            [jnp.where(c == 0, mine, part), jnp.where(c == 0, part, mine)], axis=0
        )
        x[par, y, zz, :, pl.ds(pl.multiple_of(col + c * width, 128), width)] = both.astype(
            jnp.bfloat16
        )

    put(0, hs2, sh_ref, xg[:, :hs2])
    put(hs, ht2, th_ref, xg[:, hs2:])

    def cols(u, order, core):
        start = (core * hs2, hs + core * ht2)[u] + (0 if order == 0 else widths[u][0])
        return pl.ds(pl.multiple_of(start, 128), widths[u][order])

    def span(u, core):
        start, width = ((core * hs2, hs2), (hs + core * ht2, ht2))[u]
        return pl.ds(pl.multiple_of(start, 128), width)

    def loop(lo, hi, body):
        def step(i, carry):
            body(i)
            return carry

        lax.fori_loop(lo, hi, step, 0)

    def a1(h, u, k):
        block = x.at[h, y, zz, :, cols(u, 0, c)]
        return rcopy(block, block, a1_s.at[h, u, k], a1_r.at[h, u, k], dev(0, k, 0))

    def a1_in(h, u, k):
        block = x.at[h, y, ((z - k) % NZ) // 2, :, cols(u, 0, c)]
        return rcopy(block, block, a1_s.at[h, u, k], a1_r.at[h, u, k], dev(0, k, 0))

    def a2(h, u, j):
        block = x.at[h, y, :, :, cols(u, 0, c)]
        return rcopy(block, block, a2_s.at[h, u, j], a2_r.at[h, u, j], dev(j, 0, 0))

    def a2_in(h, u, j):
        block = x.at[h, (y - j) % NY, :, :, cols(u, 0, c)]
        return rcopy(block, block, a2_s.at[h, u, j], a2_r.at[h, u, j], dev(j, 0, 0))

    def b1(h, u, j):
        block = x.at[h, y, zz, :, cols(u, 1, c)]
        return rcopy(block, block, b1_s.at[h, u, j], b1_r.at[h, u, j], dev(j, 0, 0))

    def b1_in(h, u, j):
        block = x.at[h, (y - j) % NY, zz, :, cols(u, 1, c)]
        return rcopy(block, block, b1_s.at[h, u, j], b1_r.at[h, u, j], dev(j, 0, 0))

    def b2(h, u, k):
        block = x.at[h, :, zz, :, cols(u, 1, c)]
        return rcopy(block, block, b2_s.at[h, u, k], b2_r.at[h, u, k], dev(0, k, 0))

    def b2_in(h, u, k):
        block = x.at[h, :, ((z - k) % NZ) // 2, :, cols(u, 1, c)]
        return rcopy(block, block, b2_s.at[h, u, k], b2_r.at[h, u, k], dev(0, k, 0))

    def sib(h, u, core):
        block = x.at[h, :, :, :, span(u, core)]
        return rcopy(block, block, sib_s.at[h, u], sib_r.at[h, u], dev(0, 0, 1))

    def from_parity(h, body):
        first = jnp.where(par == h, 2, 1)
        count = jnp.where(par == h, HZ - 1, HZ)
        loop(0, count, lambda i: body(first + 2 * i))

    def send_first(h, u):
        @pl.when(par == h)
        def _():
            loop(1, NZ, lambda k: a1(h, u, k).start())
            loop(1, NY, lambda j: b1(h, u, j).start())

    def send_second(h, u):
        from_parity(h, lambda k: a1_in(h, u, k).wait_recv())
        loop(1, NY, lambda j: a2(h, u, j).start())

        @pl.when(par == h)
        def _():
            loop(1, NY, lambda j: b1_in(h, u, j).wait_recv())
            loop(1, NZ, lambda k: b2(h, u, k).start())

    def send_sibling(h, u):
        loop(1, NY, lambda j: a2_in(h, u, j).wait_recv())
        from_parity(h, lambda k: b2_in(h, u, k).wait_recv())
        sib(h, u, c).start()

    def student(h):
        sib(h, 0, 1 - c).wait_recv()
        rows = x[h, :, :, :, :hs].reshape(HALF, hs)

        def tile(i):
            at = pl.ds(pl.multiple_of(i * TILE, TILE), TILE)
            logit_s[h, :, at] = jnp.dot(rows, ws[:, at], preferred_element_type=jnp.float32)

        loop(0, vs // TILE, tile)

    def teacher(h):
        sib(h, 1, 1 - c).wait_recv()
        rows = x[h, :, :, :, hs:].reshape(HALF, ht)

        def tile(i):
            at = pl.ds(pl.multiple_of(i * TILE, TILE), TILE)
            logit_t[h, :, at] = jnp.dot(rows, wt[:, at], preferred_element_type=jnp.float32)

        loop(0, vs // TILE, tile)

    lane = lax.broadcasted_iota(jnp.int32, (1, 128), 1)

    def stats(h):
        def part(i):
            at = pl.ds(pl.multiple_of(i * 32, 32), 32)
            s, t = logit_s[h, at, :], logit_t[h, at, :]
            peak_s = jnp.max(s, axis=1, keepdims=True)
            peak_t = jnp.max(t, axis=1, keepdims=True)
            e = jnp.exp(s - peak_s)
            ratio = s - t
            logit_s[h, at, :] = e
            logit_t[h, at, :] = ratio
            sum_s = jnp.sum(e, axis=1, keepdims=True)
            cross = jnp.sum(e * ratio, axis=1, keepdims=True)
            sum_t = jnp.sum(jnp.exp(t - peak_t), axis=1, keepdims=True)
            packed = jnp.where(lane == 0, peak_s, 0.0)
            for n, value in enumerate((sum_s, cross, peak_t, sum_t)):
                packed = jnp.where(lane == n + 1, value, packed)
            stat_col[h, at, :] = packed

        loop(0, HALF // 32, part)
        stat_own[h] = jnp.transpose(stat_col[h])[:8, :]

    def sz(h, k):
        return rcopy(stat_own.at[h], stat_z.at[h, k], sz_s.at[h, k], sz_r.at[h, k], dev(0, k, 0))

    def sy(h, n):
        j, d = n // NC, n % NC
        return rcopy(stat_mid.at[h], stat_y.at[h, n], sy_s.at[h, n], sy_r.at[h, n], dev(j, 0, d))

    def merge(blocks):
        peak_s = functools.reduce(jnp.maximum, [b[0:1] for b in blocks])
        peak_t = functools.reduce(jnp.maximum, [b[3:4] for b in blocks])
        sum_s = cross = sum_t = 0.0
        for b in blocks:
            scale = jnp.exp(b[0:1] - peak_s)
            sum_s = sum_s + scale * b[1:2]
            cross = cross + scale * b[2:3]
            sum_t = sum_t + jnp.exp(b[3:4] - peak_t) * b[4:5]
        return peak_s, sum_s, cross, peak_t, sum_t

    def stats_z(h):
        loop(1, NZ, lambda k: sz(h, k).start())

    def stats_y(h):
        loop(1, NZ, lambda k: sz(h, k).wait_recv())
        rows = merge([stat_own[h]] + [stat_z[h, k] for k in range(1, NZ)])
        stat_mid[h] = jnp.concatenate(list(rows) + [jnp.zeros((3, HALF), jnp.float32)], axis=0)
        loop(1, NY * NC, lambda n: sy(h, n).start())

    def factors(h):
        loop(1, NY * NC, lambda n: sy(h, n).wait_recv())
        peak_s, sum_s, cross, peak_t, sum_t = merge(
            [stat_mid[h]] + [stat_y[h, n] for n in range(1, NY * NC)]
        )
        lse_s, lse_t = peak_s + jnp.log(sum_s), peak_t + jnp.log(sum_t)
        kl = cross / sum_s - lse_s + lse_t
        offset = lse_s - lse_t + kl
        scale = jnp.exp(stat_own[h][0:1] - lse_s)
        packed = jnp.concatenate(
            [scale, offset, kl, jnp.zeros((125, HALF), jnp.float32)], axis=0
        )
        fac[h] = jnp.transpose(packed)

    def grad_rows(h):
        w = wcol[:, :, h, :, 0:1].reshape(HALF, 1)
        scale, offset = fac[h, :, 0:1] * w, fac[h, :, 1:2]
        return (scale * logit_s[h] * (logit_t[h] - offset)).astype(jnp.bfloat16)

    def back(h, grad, core, i):
        at = pl.ds(pl.multiple_of(core * hs2 + i * (hs2 // 2), 128), hs2 // 2)
        return lax.dot_general(
            grad, ws[at, :], (((1,), (1,)), ((), ())), preferred_element_type=jnp.float32
        )

    def swap(h):
        return rcopy(ps.at[h], pr.at[h], ps_s.at[h], ps_r.at[h], dev(0, 0, 1))

    def ra1(h, j):
        return rcopy(
            r1.at[h, (y + j) % NY, :, :, pl.ds(0, sa)], ra.at[h, j],
            ra1_s.at[h, j], ra1_r.at[h, j], dev(j, 0, 0),
        )

    def rb1(h, k):
        return rcopy(
            r1.at[h, :, ((z + k) % NZ) // 2, :, pl.ds(sa, hs2 - sa)], rb.at[h, k],
            rb1_s.at[h, k], rb1_r.at[h, k], dev(0, k, 0),
        )

    def rra2(h, k):
        return rcopy(
            r2a.at[h, ((z + k) % NZ) // 2], ra2.at[h, k],
            ra2_s.at[h, k], ra2_r.at[h, k], dev(0, k, 0),
        )

    def rrb2(h, j):
        return rcopy(
            r2b.at[h, (y + j) % NY], rb2.at[h, j],
            rb2_s.at[h, j], rb2_r.at[h, j], dev(j, 0, 0),
        )

    def to_parity(h, body):
        from_parity(h, body)

    def backward(h):
        grad = grad_rows(h)
        width = hs2 // 2

        for i in range(2):
            ps[h, :, i * width:(i + 1) * width] = back(h, grad, 1 - c, i)
        swap(h).start()
        for i in range(2):
            pr_at = slice(i * width, (i + 1) * width)
            fin[:, :, :, pr_at] = back(h, grad, c, i).reshape(NY, HZ, BLK, width)
        swap(h).wait_recv()
        total = fin[...] + pr[h].reshape(NY, HZ, BLK, hs2)
        r1[h] = total.astype(jnp.bfloat16)
        loop(1, NY, lambda j: ra1(h, j).start())
        to_parity(h, lambda k: rb1(h, k).start())

    def reduce_second(h):
        loop(1, NY, lambda j: ra1(h, j).wait_recv())
        total = r1[h, y, :, :, :sa].astype(jnp.float32)
        for j in range(1, NY):
            total = total + ra[h, j].astype(jnp.float32)
        r2a[h] = total.astype(jnp.bfloat16)
        to_parity(h, lambda k: rra2(h, k).start())

        @pl.when(par == h)
        def _():
            loop(1, NZ, lambda k: rb1(h, k).wait_recv())
            total = r1[h, :, zz, :, sa:].astype(jnp.float32)
            for k in range(1, NZ):
                total = total + rb[h, k].astype(jnp.float32)
            r2b[h] = total.astype(jnp.bfloat16)
            loop(1, NY, lambda j: rrb2(h, j).start())

    def final(h):
        @pl.when(par == h)
        def _():
            loop(1, NZ, lambda k: rra2(h, k).wait_recv())
            loop(1, NY, lambda j: rrb2(h, j).wait_recv())
            left = r2a[h, zz].astype(jnp.float32)
            for k in range(1, NZ):
                left = left + ra2[h, k].astype(jnp.float32)
            right = r2b[h, y].astype(jnp.float32)
            for j in range(1, NY):
                right = right + rb2[h, j].astype(jnp.float32)
            fin[0, 0, :, :sa] = left
            fin[0, 0, :, sa:] = right
            give = rcopy(
                fin.at[0, 0, pl.ds(pl.multiple_of((1 - c) * 8, 8), 8), :], fin_in,
                fin_s, fin_r, dev(0, 0, 1),
            )
            give.start()
            mine = pl.ds(pl.multiple_of(c * hs2, 128), hs2)
            theirs = pl.ds(pl.multiple_of((1 - c) * hs2, 128), hs2)
            out_ref[:, mine] = fin[0, 0, pl.ds(pl.multiple_of(c * 8, 8), 8), :]
            at = pl.multiple_of((y * HZ + zz) * BLK + c * 8, 8)
            kl_ref[...] = fac[h, pl.ds(at, 8), :]
            give.wait()
            out_ref[:, theirs] = fin_in[...]

    send_first(0, 0)
    send_first(0, 1)
    send_second(0, 0)
    send_first(1, 0)
    send_second(0, 1)
    send_first(1, 1)
    send_second(1, 0)
    send_sibling(0, 0)
    load_s.wait()
    student(0)
    send_second(1, 1)
    send_sibling(0, 1)
    load_t.wait()
    teacher(0)
    stats(0)
    stats_z(0)
    send_sibling(1, 0)
    student(1)
    stats_y(0)
    send_sibling(1, 1)
    teacher(1)
    stats(1)
    stats_z(1)
    factors(0)
    backward(0)
    stats_y(1)
    reduce_second(0)
    factors(1)
    backward(1)
    reduce_second(1)
    final(0)
    final(1)

    for h in range(2):
        for u in range(2):
            @pl.when(par == h)
            def _():
                loop(1, NZ, lambda k: a1(h, u, k).wait_send())
                loop(1, NY, lambda j: b1(h, u, j).wait_send())
                loop(1, NZ, lambda k: b2(h, u, k).wait_send())

            loop(1, NY, lambda j: a2(h, u, j).wait_send())
            sib(h, u, c).wait_send()
        loop(1, NZ, lambda k: sz(h, k).wait_send())
        loop(1, NY * NC, lambda n: sy(h, n).wait_send())
        swap(h).wait_send()
        loop(1, NY, lambda j: ra1(h, j).wait_send())
        to_parity(h, lambda k: rb1(h, k).wait_send())
        to_parity(h, lambda k: rra2(h, k).wait_send())

        @pl.when(par == h)
        def _():
            loop(1, NY, lambda j: rrb2(h, j).wait_send())


def local(student_hidden, teacher_hidden, student_head, teacher_head, segment_ids, valid_mask):
    rows, hs = student_hidden.shape
    ht = teacher_hidden.shape[1]
    vs = student_head.shape[1]
    tokens = segment_ids.shape[0]
    hs2 = hs // 2
    sa = (hs2 * 4 // 5) // 128 * 128
    f32, bf16 = jnp.float32, jnp.bfloat16
    dma = pltpu.SemaphoreType.DMA
    vmem = pl.BlockSpec(memory_space=pltpu.VMEM)
    hbm = pl.BlockSpec(memory_space=pl.ANY)
    flops = 2 * tokens * vs * (2 * hs + ht)
    kl, grad = pl.pallas_call(
        functools.partial(kernel, hs, ht, vs),
        out_shape=(
            jax.ShapeDtypeStruct((rows, 128), f32),
            jax.ShapeDtypeStruct((rows, hs), f32),
        ),
        in_specs=[vmem, vmem, vmem, vmem, hbm, hbm],
        out_specs=(vmem, vmem),
        scratch_shapes=[
            pltpu.VMEM((hs, vs), bf16),
            pltpu.VMEM((ht, vs), bf16),
            pltpu.VMEM((2, NY, HZ, BLK, hs + ht), bf16),
            pltpu.VMEM((rows, (hs + ht) // 2), f32),
            pltpu.VMEM((rows, (hs + ht) // 2), f32),
            pltpu.VMEM((2, HALF, vs), f32),
            pltpu.VMEM((2, HALF, vs), f32),
            pltpu.VMEM((2, HALF, 128), f32),
            pltpu.VMEM((2, 8, HALF), f32),
            pltpu.VMEM((2, NZ, 8, HALF), f32),
            pltpu.VMEM((2, 8, HALF), f32),
            pltpu.VMEM((2, NY * NC, 8, HALF), f32),
            pltpu.VMEM((2, HALF, 128), f32),
            pltpu.VMEM((NY, HZ, 2, BLK, 128), f32),
            pltpu.VMEM((2, HALF, hs2), f32),
            pltpu.VMEM((2, HALF, hs2), f32),
            pltpu.VMEM((2, NY, HZ, BLK, hs2), bf16),
            pltpu.VMEM((2, NY, HZ, BLK, sa), bf16),
            pltpu.VMEM((2, HZ, BLK, sa), bf16),
            pltpu.VMEM((2, NZ, BLK, sa), bf16),
            pltpu.VMEM((2, NZ, NY, BLK, hs2 - sa), bf16),
            pltpu.VMEM((2, NY, BLK, hs2 - sa), bf16),
            pltpu.VMEM((2, NY, BLK, hs2 - sa), bf16),
            pltpu.VMEM((NY, HZ, BLK, hs2), f32),
            pltpu.VMEM((8, hs2), f32),
            dma((2,)), dma(()), dma(()),
            dma((2, 2, NZ)), dma((2, 2, NZ)), dma((2, 2, NY)), dma((2, 2, NY)),
            dma((2, 2, NY)), dma((2, 2, NY)), dma((2, 2, NZ)), dma((2, 2, NZ)),
            dma((2, 2)), dma((2, 2)),
            dma((2, NZ)), dma((2, NZ)), dma((2, NY * NC)), dma((2, NY * NC)),
            dma((2,)), dma((2,)),
            dma((2, NY)), dma((2, NY)), dma((2, NZ)), dma((2, NZ)),
            dma((2, NZ)), dma((2, NZ)), dma((2, NY)), dma((2, NY)),
            dma(()), dma(()),
        ],
        compiler_params=pltpu.CompilerParams(
            collective_id=0, has_side_effects=True, vmem_limit_bytes=56 * 1024 * 1024
        ),
        cost_estimate=pl.CostEstimate(
            flops=flops, bytes_accessed=2 * vs * (hs + ht), transcendentals=2 * tokens * vs
        ),
    )(
        student_hidden, teacher_hidden,
        segment_ids.reshape(1, tokens), valid_mask.reshape(1, tokens),
        student_head, teacher_head,
    )
    return kl[:, 2], grad.astype(jnp.bfloat16)


def solution(mesh):
    in_specs = (
        P(("dp", "vocab"), None),
        P(("dp", "vocab"), None),
        P("dp", "vocab"),
        P("dp", "vocab"),
        P("dp"),
        P("dp"),
    )
    out_specs = (P(("dp", "vocab")), P(("dp", "vocab"), None))
    return jax.shard_map(local, mesh=mesh, in_specs=in_specs, out_specs=out_specs, check_vma=False)
```

time: 591 us -> 90.5 us (0.15); the launches traced: 584 us -> 90.3 us
  waiting for transfers between devices: 289 us -> 0 us
  blocking collectives: 248 us -> 0 us
  Pallas kernels: 0 us -> 86.7 us
  matrix products: 24.8 us -> 0 us
  between operations: 13.8 us -> 0.64 us
  other arithmetic: 8.6 us -> 1.51 us
    all_gather x2 -> x0, waiting for transfers between devices: 149 us -> none  [the longest x1 78.5 us: local(): lax.all_gather(teacher_hidden, 'vocab', axis=0, tiled=True)]
    reduce_scatter x1 -> x0, waiting for transfers between devices: 138 us -> none  [local(): lax.psum_scatter(lax.dot_general(grad_logits, student_head, (((1,), (1,))...]
    psum x1 -> x0, blocking collectives: 128 us -> none  [local(): lax.psum((jnp.sum(student_exp, axis=1), jnp.sum(teacher_exp, axis=1), jnp...]
    pmax x1 -> x0, blocking collectives: 120 us -> none  [local(): lax.pmax((jnp.max(part_student, axis=1), jnp.max(part_teacher, axis=1)),...]
    pallas_call x0 -> x1, Pallas kernels: none -> 86.7 us  [local(): pl.pallas_call(functools.partial(kernel, hs, ht, vs), out_shape=(jax.Shap...]
    dot_general x3 -> x0, matrix products: 24.8 us -> none  [the longest x1 9.87 us: local(): lax.dot_general(grad_logits, student_head, (((1,), (1,)), ((), ())), pref...]
  transfers between devices with their start and end apart: 3 -> 0, of which waited for: 3 -> 0; matrix products, arithmetic and copies ran while one was open for 2% -> 0% of each run, Pallas kernels for 0% -> 0%
where the time goes in v1:
time: 90.5 us; the launch traced here: 90.3 us
  Pallas kernels  86.7 us (96%)
  other arithmetic  1.51 us (2%)
  local copies, waits for them, and re-layouts  1.37 us (2%)
    pallas_call x1, Pallas kernels, local(): pl.pallas_call(functools.partial(kernel, hs, ht, vs), out_shape=(jax.Shap...  86.7 us

profile of v1, /device:TPU:37, one launch (start us, length us, event | category | flops | bytes accessed | tf_op | source)
XLA Modules:
  0.0 90.3 jit_solution(13958995535397729477)
XLA Ops:
  0.6 86.7 %shard_map.77 = (f32[8,128]{1,0:T(8,128)}, f32[8,2560]{1,0:T(8,128)}) custom-call(bf16[8,2560]{1,0:T(8,128)(2,1)} %sh_ref.1, bf16[8,2048]{1,0:T(8,128)(2,1)} %th_ref.1, s32[1,512]{1,0:T(1,128)} %bitcast.2, s32[1,512]{1,0:T(1,128)} %bitcast.3, bf16[2560,1280]{1,0:T(8,128)(2,1)} %ws_hbm.1, bf16[2048,1280]{1,0:T(8,128)(2,1)} %wt_hbm.1), custom_call_target="tpu_custom_call" | custom-call | flops 9395240960 | bytes 11796480 | tf_op jit(solution)/shard_map/pallas_call | solution.py:412
  87.4 1.4 %slice_reduce_fusion = f32[8]{0:T(128)} fusion(f32[8,128]{1,0:T(8,128)} %get-tuple-element.4), kind=kLoop, calls=%fused_computation | loop fusion | bytes 64 | tf_op jit(solution)/shard_map/slice | solution.py:467
  88.8 1.5 %convert_element_type.3 = bf16[8,2560]{1,0:T(8,128)(2,1)} convert(f32[8,2560]{1,0:T(8,128)} %get-tuple-element.5) | non-fusion elementwise | flops 20480 | bytes 122880 | tf_op jit(solution)/shard_map/convert_element_type | solution.py:467

commit v2 on v1

v2 whole, which is shorter than its diff:
```python
import functools

import jax
import jax.numpy as jnp
from jax import lax
from jax.experimental import pallas as pl
from jax.experimental.pallas import tpu as pltpu
from jax.sharding import PartitionSpec as P

LOSS_SCALE = 1024.0
NY, NZ, NC = 4, 8, 2
N = 2
HZ = NZ // N
BLK = 16
ROWS = NY * HZ * BLK
TILE = 256
GROUP, PART = 128, 32
SPLIT_S, SPLIT_T, SPLIT_G = 1024, 768, 896
MESH = pl.DeviceIdType.MESH


def kernel(
    hs, ht, vs,
    sh_ref, th_ref, seg_ref, valid_ref, ws_hbm, wt_hbm,
    out_ref,
    ws, wst, wt, x, xf, xg, logit_s, logit_t, exp_s,
    ab, stat_col, stat_own, stat_z, stat_mid, stat_y, fac, wcol,
    gb_rows, ps, pr, r1, ra, r2a, ra2, rb, r2b, rb2, fin, fin_in,
    load_sem, pair_s, pair_r,
    a1_s, a1_r, a2_s, a2_r, b1_s, b1_r, b2_s, b2_r, sib_s, sib_r,
    sz_s, sz_r, sy_s, sy_r, ps_s, ps_r,
    ra1_s, ra1_r, ra2_s, ra2_r, rb1_s, rb1_r, rb2_s, rb2_r, fin_s, fin_r,
):
    v = lax.axis_index("vocab")
    y, z, c = v // (NZ * NC), (v // NC) % NZ, v % NC
    zz, own = z // N, z % N
    hs2, ht2 = hs // 2, ht // 2
    sa, ta = SPLIT_S, SPLIT_T
    ga = SPLIT_G
    gb = hs2 - ga
    widths = ((sa, hs2 - sa), (ta, ht2 - ta))

    def dev(dy, dz, dc):
        return {"vocab": (((y + dy) % NY) * NZ + (z + dz) % NZ) * NC + (c + dc) % NC}

    def rcopy(src, dst, ssem, rsem, device):
        return pltpu.make_async_remote_copy(
            src_ref=src, dst_ref=dst, send_sem=ssem, recv_sem=rsem,
            device_id=device, device_id_type=MESH,
        )

    load_s = pltpu.make_async_copy(ws_hbm, ws, load_sem.at[0])
    load_t = pltpu.make_async_copy(wt_hbm, wt, load_sem.at[1])
    load_s.start()
    load_t.start()

    barrier = pltpu.get_barrier_semaphore()
    partners = [(0, k, 0) for k in range(1, NZ)]
    partners += [(j, 0, d) for j in range(1, NY) for d in range(NC)] + [(0, 0, 1)]
    for p in partners:
        pl.semaphore_signal(barrier, inc=1, device_id=dev(*p), device_id_type=MESH)
    xf[:, :hs2] = sh_ref[:, pl.ds(pl.multiple_of((1 - c) * hs2, 128), hs2)].astype(jnp.float32)
    xf[:, hs2:] = th_ref[:, pl.ds(pl.multiple_of((1 - c) * ht2, 128), ht2)].astype(jnp.float32)
    pl.semaphore_wait(barrier, len(partners))
    pair = rcopy(xf, xg, pair_s, pair_r, dev(0, 0, 1))
    pair.start()

    seg = jnp.broadcast_to(seg_ref[...].astype(jnp.float32), (128, N * ROWS))
    val = jnp.broadcast_to(valid_ref[...].astype(jnp.float32), (128, N * ROWS))
    seg_c, val_c = jnp.transpose(seg)[:, :1], jnp.transpose(val)[:, :1]
    same = jnp.where(seg_c == seg[:1, :], val[:1, :], 0.0)
    count = jnp.sum(same, axis=1, keepdims=True)
    weight = LOSS_SCALE * val_c / jnp.maximum(count, 1.0)
    wcol[...] = jnp.broadcast_to(weight, (N * ROWS, 128)).reshape(NY, HZ, N, BLK, 128)

    pair.wait()

    def put(col, width, full, part):
        mine = full[:, pl.ds(pl.multiple_of(c * width, 128), width)].astype(jnp.float32)
        both = jnp.concatenate(
            [jnp.where(c == 0, mine, part), jnp.where(c == 0, part, mine)], axis=0
        )
        x[own, y, zz, :, pl.ds(pl.multiple_of(col + c * width, 128), width)] = both.astype(
            jnp.bfloat16
        )

    put(0, hs2, sh_ref, xg[:, :hs2])
    put(hs, ht2, th_ref, xg[:, hs2:])

    def cols(u, order, core):
        start = (core * hs2, hs + core * ht2)[u] + (0 if order == 0 else widths[u][0])
        return pl.ds(pl.multiple_of(start, 128), widths[u][order])

    def span(u, core):
        start, width = ((core * hs2, hs2), (hs + core * ht2, ht2))[u]
        return pl.ds(pl.multiple_of(start, 128), width)

    def loop(lo, hi, body):
        def step(i, carry):
            body(i)
            return carry

        lax.fori_loop(lo, hi, step, 0)

    def a1(h, u, k):
        block = x.at[h, y, zz, :, cols(u, 0, c)]
        return rcopy(block, block, a1_s.at[u], a1_r.at[h, u, zz], dev(0, k, 0))

    def a2(h, u, b, j):
        block = x.at[h, y, b, :, cols(u, 0, c)]
        return rcopy(block, block, a2_s.at[u], a2_r.at[h, u], dev(j, 0, 0))

    def b1(h, u, j):
        block = x.at[h, y, zz, :, cols(u, 1, c)]
        return rcopy(block, block, b1_s.at[u], b1_r.at[u], dev(j, 0, 0))

    def b2(h, u, k):
        block = x.at[h, :, zz, :, cols(u, 1, c)]
        return rcopy(block, block, b2_s.at[u], b2_r.at[h, u], dev(0, k, 0))

    def sib(h, u, order):
        block = x.at[h, :, :, :, cols(u, order, c)]
        return rcopy(block, block, sib_s.at[u], sib_r.at[h, u], dev(0, 0, 1))

    flat = x.reshape(N * ROWS, hs + ht)

    def arrived(sem, rows, width):
        some = flat.at[pl.ds(0, rows), pl.ds(0, width)]
        pltpu.make_async_copy(some, some, sem).wait()

    def arrived_f32(sem, like):
        pltpu.make_async_copy(like, like, sem).wait()

    def near_first(k0, count, step, body):
        def some(i):
            k = k0 + step * (i // 2)
            body(jnp.where(i % 2 == 0, k, NZ - k))

        loop(0, count, some)

    def behind(h, body):
        near_first(
            jnp.where(own == h, 2, 1), jnp.where(own == h, HZ - 1, HZ), N, body
        )

    ahead = behind

    def send_first(h, u):
        @pl.when(own == h)
        def _():
            loop(1, NY, lambda j: b1(h, u, j).start())
            near_first(1, NZ - 1, 1, lambda k: a1(h, u, k).start())
            loop(1, NY, lambda j: a2(h, u, zz, j).start())

    def relay(h, u):
        @pl.when(own == h)
        def _():
            arrived(b1_r.at[u], (NY - 1) * BLK, widths[u][1])
            near_first(1, NZ - 1, 1, lambda k: b2(h, u, k).start())

        def onward(k):
            b = ((z - k + NZ) % NZ) // N
            arrived(a1_r.at[h, u, b], BLK, widths[u][0])
            loop(1, NY, lambda j: a2(h, u, b, j).start())

        behind(h, onward)

    def send_sibling(h, u):
        arrived(a2_r.at[h, u], (NY - 1) * HZ * BLK, widths[u][0])
        sib(h, u, 0).start()

        @pl.when(own == h)
        def _():
            arrived(b2_r.at[h, u], (HZ - 1) * NY * BLK, widths[u][1])

        @pl.when(own != h)
        def _():
            arrived(b2_r.at[h, u], HZ * NY * BLK, widths[u][1])

        sib(h, u, 1).start()

    def gathered(u):
        for h in range(N):
            arrived(sib_r.at[h, u], ROWS, (hs2, ht2)[u])

    def student():
        def tile(i):
            at = pl.ds(pl.multiple_of(i * TILE, TILE), TILE)
            rows = x[:, :, :, :, :hs].reshape(N * ROWS, hs)
            logits = jnp.dot(rows, ws[:, at], preferred_element_type=jnp.float32)
            logit_s[:, :, at] = logits.reshape(N, ROWS, TILE)

        loop(0, vs // TILE, tile)

    def teacher():
        def tile(i):
            at = pl.ds(pl.multiple_of(i * TILE, TILE), TILE)
            rows = x[:, :, :, :, hs:].reshape(N * ROWS, ht)
            logits = jnp.dot(rows, wt[:, at], preferred_element_type=jnp.float32)
            logit_t[:, :, at] = logits.reshape(N, ROWS, TILE)

        loop(0, vs // TILE, tile)

    lane = lax.broadcasted_iota(jnp.int32, (1, 128), 1)

    def groups(body):
        def some(i):
            for n in range(GROUP // PART):
                body(pl.ds(pl.multiple_of(i * GROUP + n * PART, PART), PART))

        loop(0, ROWS // GROUP, some)

    def stats_s(h):
        def some(at):
            s = logit_s[h, at, :]
            peak = jnp.max(s, axis=1, keepdims=True)
            e = jnp.exp(s - peak)
            exp_s[h, at, :] = e
            total = jnp.sum(e, axis=1, keepdims=True)
            stat_col[h, at, :] = jnp.where(lane == 0, peak, jnp.where(lane == 1, total, 0.0))

        groups(some)

    def stats_t(h):
        def some(at):
            t = logit_t[h, at, :]
            peak = jnp.max(t, axis=1, keepdims=True)
            total = jnp.sum(jnp.exp(t - peak), axis=1, keepdims=True)
            cross = jnp.sum(exp_s[h, at, :] * (logit_s[h, at, :] - t), axis=1, keepdims=True)
            packed = stat_col[h, at, :]
            mean = cross / packed[:, 1:2]
            for m, value in enumerate((cross, peak, total, mean)):
                packed = jnp.where(lane == m + 2, value, packed)
            stat_col[h, at, :] = packed

        groups(some)

    def sz(h, k):
        return rcopy(stat_own.at[h], stat_z.at[h, k], sz_s, sz_r.at[h], dev(0, k, 0))

    def sy(h, n):
        j, d = n // NC, n % NC
        return rcopy(stat_mid.at[h], stat_y.at[h, n], sy_s, sy_r.at[h], dev(j, 0, d))

    def merge(blocks):
        peak_s = functools.reduce(jnp.maximum, [b[0:1] for b in blocks])
        peak_t = functools.reduce(jnp.maximum, [b[3:4] for b in blocks])
        sum_s = cross = sum_t = 0.0
        for b in blocks:
            scale = jnp.exp(b[0:1] - peak_s)
            sum_s = sum_s + scale * b[1:2]
            cross = cross + scale * b[2:3]
            sum_t = sum_t + jnp.exp(b[3:4] - peak_t) * b[4:5]
        return peak_s, sum_s, cross, peak_t, sum_t

    def stats_z(h):
        stat_own[h] = jnp.transpose(stat_col[h])[:8, :]
        loop(1, NZ, lambda k: sz(h, k).start())

    def stats_y(h):
        arrived_f32(sz_r.at[h], stat_z.at[h, pl.ds(1, NZ - 1)])
        rows = merge([stat_own[h]] + [stat_z[h, k] for k in range(1, NZ)])
        stat_mid[h] = jnp.concatenate(list(rows) + [jnp.zeros((3, ROWS), jnp.float32)], axis=0)
        loop(1, NY * NC, lambda n: sy(h, n).start())

    def factors(h):
        arrived_f32(sy_r.at[h], stat_y.at[h, pl.ds(1, NY * NC - 1)])
        peak_s, sum_s, cross, peak_t, sum_t = merge(
            [stat_mid[h]] + [stat_y[h, n] for n in range(1, NY * NC)]
        )
        lse_s, lse_t = peak_s + jnp.log(sum_s), peak_t + jnp.log(sum_t)
        kl = cross / sum_s - lse_s + lse_t
        offset = lse_s - lse_t + kl
        scale = jnp.exp(stat_own[h][0:1] - lse_s)
        local_mean = stat_own[h][5:6]
        packed = jnp.concatenate(
            [scale, offset - local_mean, kl, jnp.zeros((125, ROWS), jnp.float32)], axis=0
        )
        fac[h] = jnp.transpose(packed)

    def grads(h):
        def some(at):
            e = exp_s[h, at, :]
            ratio = logit_s[h, at, :] - logit_t[h, at, :]
            gb_rows[at, :] = (e * (ratio - stat_col[h, at, 5:6])).astype(jnp.bfloat16)
            gb_rows[pl.ds(ROWS + at.start, PART), :] = e.astype(jnp.bfloat16)

        groups(some)

    part = hs2 // 2

    def transpose(lo, hi):
        def block(i):
            at = pl.ds(pl.multiple_of(i * TILE, TILE), TILE)
            wst[:, at] = jnp.transpose(ws[at, :])

        loop(lo, hi, block)

    def back(h, lo, hi):
        def block(i):
            at = pl.ds(pl.multiple_of(i * 2 * TILE, 2 * TILE), 2 * TILE)
            ab[h, :, at] = jnp.dot(
                gb_rows[...], wst[:, at], preferred_element_type=jnp.float32
            )

        loop(lo, hi, block)

    def mixed(h, core, i):
        w = wcol[:, :, h, :, 0:1].reshape(ROWS, 1)
        at = pl.ds(pl.multiple_of(core * hs2 + i * part, 128), part)
        scale, offset = fac[h, :, 0:1] * w, fac[h, :, 1:2]
        return scale * (ab[h, :ROWS, at] - offset * ab[h, ROWS:, at])

    def swap(h, i):
        return rcopy(ps.at[h, i], pr.at[h, i], ps_s, ps_r.at[h, i], dev(0, 0, 1))

    def ra1(h, j):
        return rcopy(
            r1.at[h, (y + j) % NY, :, :, pl.ds(0, ga)], ra.at[h, j],
            ra1_s, ra1_r.at[h], dev(j, 0, 0),
        )

    def rb1(h, k):
        return rcopy(
            r1.at[h, :, ((z + k) % NZ) // N, :, pl.ds(ga, gb)], rb.at[h, k],
            rb1_s, rb1_r, dev(0, k, 0),
        )

    def rra2(h, k):
        return rcopy(
            r2a.at[h, ((z + k) % NZ) // N], ra2.at[h, k],
            ra2_s, ra2_r, dev(0, k, 0),
        )

    def rrb2(h, j):
        return rcopy(
            r2b.at[h, (y + j) % NY], rb2.at[h, j],
            rb2_s, rb2_r, dev(j, 0, 0),
        )

    def mix(h):
        for i in range(2):
            ps[h, i] = mixed(h, 1 - c, i)
            swap(h, i).start()

    def reduce_first(h):
        for i in range(2):
            total = mixed(h, c, i)
            swap(h, i).wait_recv()
            total = total + pr[h, i]
            r1[h, :, :, :, i * part:(i + 1) * part] = (
                total.astype(jnp.bfloat16).reshape(NY, HZ, BLK, part)
            )
        loop(1, NY, lambda j: ra1(h, j).start())
        ahead(h, lambda k: rb1(h, k).start())

    def reduce_second(h):
        arrived(ra1_r.at[h], (NY - 1) * HZ * BLK, ga)
        total = r1[h, y, :, :, :ga].astype(jnp.float32)
        for j in range(1, NY):
            total = total + ra[h, j].astype(jnp.float32)
        r2a[h] = total.astype(jnp.bfloat16)
        ahead(h, lambda k: rra2(h, k).start())

        @pl.when(own == h)
        def _():
            arrived(rb1_r, (NZ - 1) * NY * BLK, gb)
            total = r1[h, :, zz, :, ga:].astype(jnp.float32)
            for k in range(1, NZ):
                total = total + rb[h, k].astype(jnp.float32)
            r2b[h] = total.astype(jnp.bfloat16)
            loop(1, NY, lambda j: rrb2(h, j).start())

    def final(h):
        @pl.when(own == h)
        def _():
            arrived(ra2_r, (NZ - 1) * BLK, ga)
            arrived(rb2_r, (NY - 1) * BLK, gb)
            left = r2a[h, zz].astype(jnp.float32)
            for k in range(1, NZ):
                left = left + ra2[h, k].astype(jnp.float32)
            right = r2b[h, y].astype(jnp.float32)
            for j in range(1, NY):
                right = right + rb2[h, j].astype(jnp.float32)
            fin[:, :ga] = left
            fin[:, ga:] = right
            give = rcopy(
                fin.at[pl.ds(pl.multiple_of((1 - c) * 8, 8), 8), :], fin_in,
                fin_s, fin_r, dev(0, 0, 1),
            )
            give.start()
            mine = pl.ds(pl.multiple_of(c * hs2, 128), hs2)
            theirs = pl.ds(pl.multiple_of((1 - c) * hs2, 128), hs2)
            out_ref[:, mine] = fin[pl.ds(pl.multiple_of(c * 8, 8), 8), :]
            at = pl.multiple_of((y * HZ + zz) * BLK + c * 8, 8)
            kl = fac[h, pl.ds(at, 8), 2:3]
            row = lax.broadcasted_iota(jnp.int32, (8, 128), 0)
            col = lax.broadcasted_iota(jnp.int32, (8, 128), 1)
            kl = jnp.sum(jnp.where(row == col, kl, 0.0), axis=0, keepdims=True)
            out_ref[:, hs:] = jnp.broadcast_to(kl, (8, 128))
            give.wait()
            out_ref[:, theirs] = fin_in[...]

    def gather_left():
        for u in range(2):
            arrived(a1_s.at[u], (NZ - 1) * BLK, widths[u][0])
            arrived(b1_s.at[u], (NY - 1) * BLK, widths[u][1])
            arrived(b2_s.at[u], (NZ - 1) * NY * BLK, widths[u][1])
            arrived(a2_s.at[u], (NY - 1) * N * HZ * BLK, widths[u][0])
            arrived(sib_s.at[u], N * ROWS, (hs2, ht2)[u])

    def rest_left():
        arrived_f32(sz_s, stat_z.at[:, pl.ds(1, NZ - 1)])
        arrived_f32(sy_s, stat_y.at[:, pl.ds(1, NY * NC - 1)])
        arrived_f32(ps_s, ps)
        arrived(ra1_s, N * (NY - 1) * HZ * BLK, ga)
        arrived(rb1_s, (NZ - 1) * NY * BLK, gb)
        arrived(ra2_s, (NZ - 1) * BLK, ga)
        arrived(rb2_s, (NY - 1) * BLK, gb)

    for u in range(2):
        for h in range(N):
            send_first(h, u)
    load_s.wait()
    transpose(0, hs // TILE)
    for u in range(2):
        for h in range(N):
            relay(h, u)
    load_t.wait()
    for h in range(N):
        send_sibling(h, 0)
    gathered(0)
    student()
    for h in range(N):
        stats_s(h)
    for h in range(N):
        send_sibling(h, 1)
    gathered(1)
    teacher()
    for h in range(N):
        stats_t(h)
        stats_z(h)
    grads(0)
    back(0, 0, 5)
    stats_y(0)
    stats_y(1)
    grads(1)
    back(1, 0, 5)
    factors(0)
    mix(0)
    factors(1)
    mix(1)
    reduce_first(0)
    reduce_first(1)
    reduce_second(0)
    gather_left()
    reduce_second(1)
    for h in range(N):
        final(h)
    rest_left()


def split(result_ref, kl_ref, grad_ref):
    rows, hs = grad_ref.shape
    kl_ref[...] = result_ref[:1, hs:hs + rows]
    grad_ref[...] = result_ref[:, :hs].astype(jnp.bfloat16)


def local(student_hidden, teacher_hidden, student_head, teacher_head, segment_ids, valid_mask):
    rows, hs = student_hidden.shape
    ht = teacher_hidden.shape[1]
    vs = student_head.shape[1]
    tokens = segment_ids.shape[0]
    hs2 = hs // 2
    ga, gb = SPLIT_G, hs2 - SPLIT_G
    f32, bf16 = jnp.float32, jnp.bfloat16
    dma = pltpu.SemaphoreType.DMA
    vmem = pl.BlockSpec(memory_space=pltpu.VMEM)
    hbm = pl.BlockSpec(memory_space=pl.ANY)
    flops = 2 * tokens * vs * (2 * hs + ht)
    result = pl.pallas_call(
        functools.partial(kernel, hs, ht, vs),
        out_shape=jax.ShapeDtypeStruct((rows, hs + 128), f32),
        in_specs=[vmem, vmem, vmem, vmem, hbm, hbm],
        out_specs=vmem,
        scratch_shapes=[
            pltpu.VMEM((hs, vs), bf16),
            pltpu.VMEM((vs, hs), bf16),
            pltpu.VMEM((ht, vs), bf16),
            pltpu.VMEM((N, NY, HZ, BLK, hs + ht), bf16),
            pltpu.VMEM((rows, (hs + ht) // 2), f32),
            pltpu.VMEM((rows, (hs + ht) // 2), f32),
            pltpu.VMEM((N, ROWS, vs), f32),
            pltpu.VMEM((N, ROWS, vs), f32),
            pltpu.VMEM((N, ROWS, vs), f32),
            pltpu.VMEM((N, 2 * ROWS, hs), f32),
            pltpu.VMEM((N, ROWS, 128), f32),
            pltpu.VMEM((N, 8, ROWS), f32),
            pltpu.VMEM((N, NZ, 8, ROWS), f32),
            pltpu.VMEM((N, 8, ROWS), f32),
            pltpu.VMEM((N, NY * NC, 8, ROWS), f32),
            pltpu.VMEM((N, ROWS, 128), f32),
            pltpu.VMEM((NY, HZ, N, BLK, 128), f32),
            pltpu.VMEM((2 * ROWS, vs), bf16),
            pltpu.VMEM((N, 2, ROWS, hs2 // 2), f32),
            pltpu.VMEM((N, 2, ROWS, hs2 // 2), f32),
            pltpu.VMEM((N, NY, HZ, BLK, hs2), bf16),
            pltpu.VMEM((N, NY, HZ, BLK, ga), bf16),
            pltpu.VMEM((N, HZ, BLK, ga), bf16),
            pltpu.VMEM((N, NZ, BLK, ga), bf16),
            pltpu.VMEM((N, NZ, NY, BLK, gb), bf16),
            pltpu.VMEM((N, NY, BLK, gb), bf16),
            pltpu.VMEM((N, NY, BLK, gb), bf16),
            pltpu.VMEM((BLK, hs2), f32),
            pltpu.VMEM((8, hs2), f32),
            dma((2,)), dma(()), dma(()),
            dma((2,)), dma((N, 2, HZ)), dma((2,)), dma((N, 2)),
            dma((2,)), dma((2,)), dma((2,)), dma((N, 2)),
            dma((2,)), dma((N, 2)),
            dma(()), dma((N,)), dma(()), dma((N,)), dma(()), dma((N, 2)),
            dma(()), dma((N,)), dma(()), dma(()),
            dma(()), dma(()), dma(()), dma(()),
            dma(()), dma(()),
        ],
        compiler_params=pltpu.CompilerParams(
            collective_id=0, has_side_effects=True, vmem_limit_bytes=56 * 1024 * 1024
        ),
        cost_estimate=pl.CostEstimate(
            flops=flops, bytes_accessed=2 * vs * (hs + ht), transcendentals=2 * tokens * vs
        ),
    )(
        student_hidden, teacher_hidden,
        segment_ids.reshape(1, tokens), valid_mask.reshape(1, tokens),
        student_head, teacher_head,
    )
    kl, grad = pl.pallas_call(
        split,
        out_shape=(jax.ShapeDtypeStruct((1, rows), f32), jax.ShapeDtypeStruct((rows, hs), bf16)),
        in_specs=[vmem],
        out_specs=(vmem, vmem),
    )(result)
    return kl.reshape(rows), grad


def solution(mesh):
    in_specs = (
        P(("dp", "vocab"), None),
        P(("dp", "vocab"), None),
        P("dp", "vocab"),
        P("dp", "vocab"),
        P("dp"),
        P("dp"),
    )
    out_specs = (P(("dp", "vocab")), P(("dp", "vocab"), None))
    return jax.shard_map(local, mesh=mesh, in_specs=in_specs, out_specs=out_specs, check_vma=False)
```

time: 90.5 us -> 79.8 us (0.88)
  Pallas kernels: 86.7 us -> 79 us
  other arithmetic: 1.51 us -> 0 us
  local copies, waits for them, and re-layouts: 1.37 us -> 0 us
    pallas_call x1 -> x2, Pallas kernels: 86.7 us -> 79 us  [the longest x1 77.4 us: local(): pl.pallas_call(functools.partial(kernel, hs, ht, vs), out_shape=jax.Shape...]
    convert_element_type x1 -> x0, other arithmetic: 1.51 us -> none  [local(): return (kl[:, 2], grad.astype(jnp.bfloat16))]
    slice x1 -> x0, local copies, waits for them, and re-layouts: 1.37 us -> none  [local(): return (kl[:, 2], grad.astype(jnp.bfloat16))]
where the time goes in v2:
time: 79.8 us; the launch traced here: 79.6 us
  Pallas kernels  79 us (99%)
    pallas_call x1, Pallas kernels, local(): pl.pallas_call(functools.partial(kernel, hs, ht, vs), out_shape=jax.Shape...  77.4 us

profile of v2, /device:TPU:37, one launch (start us, length us, event | category | flops | bytes accessed | tf_op | source)
XLA Modules:
  0.0 79.6 jit_solution(11201714444099849695)
XLA Ops:
  0.6 77.4 %shard_map.77.result_ref = f32[8,2688]{1,0:T(8,128)} custom-call(bf16[8,2560]{1,0:T(8,128)(2,1)} %sh_ref.1, bf16[8,2048]{1,0:T(8,128)(2,1)} %th_ref.1, s32[1,512]{1,0:T(1,128)} %bitcast.3, s32[1,512]{1,0:T(1,128)} %bitcast.4, bf16[2560,1280]{1,0:T(8,128)(2,1)} %ws_hbm.1, bf16[2048,1280]{1,0:T(8,128)(2,1)} %wt_hbm.1), custom_call_target="tpu_custom_call" | custom-call | flops 9395240960 | bytes 11796480 | tf_op jit(solution)/shard_map/pallas_call | solution.py:481
  78.1 1.5 %shard_map.78 = (f32[1,8]{1,0:T(1,128)}, bf16[8,2560]{1,0:T(8,128)(2,1)}) custom-call(f32[8,2688]{1,0:T(8,128)} %shard_map.77.result_ref), custom_call_target="tpu_custom_call" | custom-call | tf_op jit(solution)/shard_map/pallas_call | solution.py:536

commit v3 on v2

--- a/solution.py
+++ b/solution.py
@@ -23,12 +23,12 @@
     hs, ht, vs,
     sh_ref, th_ref, seg_ref, valid_ref, ws_hbm, wt_hbm,
     out_ref,
-    ws, wst, wt, x, xf, xg, logit_s, logit_t, exp_s,
-    ab, stat_col, stat_own, stat_z, stat_mid, stat_y, fac, wcol,
-    gb_rows, ps, pr, r1, ra, r2a, ra2, rb, r2b, rb2, fin, fin_in,
+    ws, w_in, wst, wt, x, xf, xg, logit_s, logit_t, exp_s,
+    sum_e, sum_a, stat_col, stat_own, stat_sib, stat_z, stat_mid, stat_y, fac, wcol,
+    e_rows, e_in, a_rows, a_in, r1, ra, r2a, ra2, rb, r2b, rb2, fin, fin_in,
     load_sem, pair_s, pair_r,
-    a1_s, a1_r, a2_s, a2_r, b1_s, b1_r, b2_s, b2_r, sib_s, sib_r,
-    sz_s, sz_r, sy_s, sy_r, ps_s, ps_r,
+    a1_s, a1_r, a2_s, a2_r, a2f_r, a3_r, b1_s, b1_r, b2_s, b2_r, b2f_r, sib_s, sib_r,
+    sz_s, sz_r, sy_s, sy_r, w_s, w_r, ss_s, ss_r, ge_s, ge_r, ga_s, ga_r,
     ra1_s, ra1_r, ra2_s, ra2_r, rb1_s, rb1_r, rb2_s, rb2_r, fin_s, fin_r,
 ):
     v = lax.axis_index("vocab")
@@ -102,24 +102,43 @@
 
         lax.fori_loop(lo, hi, step, 0)
 
-    def a1(h, u, k):
-        block = x.at[h, y, zz, :, cols(u, 0, c)]
-        return rcopy(block, block, a1_s.at[u], a1_r.at[h, u, zz], dev(0, k, 0))
-
-    def a2(h, u, b, j):
+    def a1(u, k, ahead):
+        source = (z - k + NZ) % NZ
+        h, b = source % N, source // N
         block = x.at[h, y, b, :, cols(u, 0, c)]
-        return rcopy(block, block, a2_s.at[u], a2_r.at[h, u], dev(j, 0, 0))
+        return rcopy(block, block, a1_s.at[u], a1_r.at[h, u, b], dev(0, ahead, 0))
+
+    onward, back_y = jnp.where(c == 0, 1, NY - 1), jnp.where(c == 0, NY - 1, 1)
+
+    def a2_on(h, u, b, late):
+        block = x.at[h, y, b, :, cols(u, 0, c)]
+        return rcopy(block, block, a2_s.at[u], a2f_r.at[u, late], dev(onward, 0, 0))
+
+    def a2_back(h, u, b):
+        block = x.at[h, y, b, :, cols(u, 0, c)]
+        return rcopy(block, block, a2_s.at[u], a2_r.at[h, u], dev(back_y, 0, 0))
+
+    def a3(u, k):
+        source = (z - k + NZ) % NZ
+        h, b = source % N, source // N
+        block = x.at[h, (y + back_y) % NY, b, :, cols(u, 0, c)]
+        return rcopy(block, block, a2_s.at[u], a3_r.at[h, u], dev(onward, 0, 0))
 
     def b1(h, u, j):
         block = x.at[h, y, zz, :, cols(u, 1, c)]
         return rcopy(block, block, b1_s.at[u], b1_r.at[u], dev(j, 0, 0))
 
-    def b2(h, u, k):
-        block = x.at[h, :, zz, :, cols(u, 1, c)]
-        return rcopy(block, block, b2_s.at[u], b2_r.at[h, u], dev(0, k, 0))
-
-    def sib(h, u, order):
-        block = x.at[h, :, :, :, cols(u, order, c)]
+    def b2(u, k, ahead, sem):
+        source = (z - k + NZ) % NZ
+        block = x.at[source % N, :, source // N, :, cols(u, 1, c)]
+        return rcopy(block, block, b2_s.at[u], sem, dev(0, ahead, 0))
+
+    def sib_a(h, u, dy):
+        block = x.at[h, (y + dy) % NY, :, :, cols(u, 0, c)]
+        return rcopy(block, block, sib_s.at[u], sib_r.at[h, u], dev(0, 0, 1))
+
+    def sib_b(h, u):
+        block = x.at[h, :, :, :, cols(u, 1, c)]
         return rcopy(block, block, sib_s.at[u], sib_r.at[h, u], dev(0, 0, 1))
 
     flat = x.reshape(N * ROWS, hs + ht)
@@ -145,61 +164,120 @@
 
     ahead = behind
 
-    def send_first(h, u):
-        @pl.when(own == h)
+    def send_first(u):
+        loop(1, NY, lambda j: b1(own, u, j).start())
+        a1(u, 0, 1).start()
+        a1(u, 0, NZ - 1).start()
+        a2_on(own, u, zz, 0).start()
+        a2_back(own, u, zz).start()
+        a1(u, 0, 2).start()
+        a1(u, 0, NZ - 2).start()
+
+    direct, relayed = (1, NZ - 1, 2, NZ - 2), (3, NZ - 3, 4)
+
+    def relay(u, late):
+        for k in (direct, relayed)[late]:
+            source = (z - k + NZ) % NZ
+            h, b = source % N, source // N
+            arrived(a1_r.at[h, u, b], BLK, widths[u][0])
+            if k == 2:
+                a1(u, k, 1).start()
+
+                @pl.when(c == 0)
+                def _():
+                    a1(u, k, 2).start()
+
+            if k == NZ - 2:
+                a1(u, k, NZ - 1).start()
+
+                @pl.when(c == 1)
+                def _():
+                    a1(u, k, NZ - 2).start()
+
+            a2_on(h, u, b, late).start()
+            a2_back(h, u, b).start()
+
+    def relay_b(u):
+        arrived(b1_r.at[u], (NY - 1) * BLK, widths[u][1])
+        b2(u, 0, 2, b2f_r.at[u, 0]).start()
+        b2(u, 0, NZ - 2, b2f_r.at[u, 1]).start()
+        b2(u, 0, 1, b2_r.at[u]).start()
+        b2(u, 0, NZ - 1, b2_r.at[u]).start()
+
+    def relay_b2(u):
+        arrived(b2f_r.at[u, 0], NY * BLK, widths[u][1])
+        b2(u, 2, 1, b2_r.at[u]).start()
+
+        @pl.when(c == 0)
         def _():
-            loop(1, NY, lambda j: b1(h, u, j).start())
-            near_first(1, NZ - 1, 1, lambda k: a1(h, u, k).start())
-            loop(1, NY, lambda j: a2(h, u, zz, j).start())
-
-    def relay(h, u):
-        @pl.when(own == h)
+            b2(u, 2, 2, b2_r.at[u]).start()
+
+        arrived(b2f_r.at[u, 1], NY * BLK, widths[u][1])
+        b2(u, NZ - 2, NZ - 1, b2_r.at[u]).start()
+
+        @pl.when(c == 1)
         def _():
-            arrived(b1_r.at[u], (NY - 1) * BLK, widths[u][1])
-            near_first(1, NZ - 1, 1, lambda k: b2(h, u, k).start())
-
-        def onward(k):
-            b = ((z - k + NZ) % NZ) // N
-            arrived(a1_r.at[h, u, b], BLK, widths[u][0])
-            loop(1, NY, lambda j: a2(h, u, b, j).start())
-
-        behind(h, onward)
-
-    def send_sibling(h, u):
-        arrived(a2_r.at[h, u], (NY - 1) * HZ * BLK, widths[u][0])
-        sib(h, u, 0).start()
-
-        @pl.when(own == h)
-        def _():
-            arrived(b2_r.at[h, u], (HZ - 1) * NY * BLK, widths[u][1])
-
-        @pl.when(own != h)
-        def _():
-            arrived(b2_r.at[h, u], HZ * NY * BLK, widths[u][1])
-
-        sib(h, u, 1).start()
+            b2(u, NZ - 2, NZ - 2, b2_r.at[u]).start()
+
+    def relay_y(u, late):
+        ks = ((0,) + direct, relayed)[late]
+        arrived(a2f_r.at[u, late], len(ks) * BLK, widths[u][0])
+        for k in ks:
+            a3(u, k).start()
+        if late:
+            for h in range(N):
+                sib_a(h, u, back_y).start()
+
+    def send_sibling_own(u):
+        for h in range(N):
+            sib_a(h, u, 0).start()
+
+    def send_sibling_b(u):
+        arrived(b2_r.at[u], 5 * NY * BLK, widths[u][1])
+        for h in range(N):
+            sib_b(h, u).start()
+
+    def send_sibling_a(h, u):
+        arrived(a2_r.at[h, u], HZ * BLK, widths[u][0])
+        sib_a(h, u, onward).start()
+
+    def send_sibling_last(h, u):
+        arrived(a3_r.at[h, u], HZ * BLK, widths[u][0])
+        sib_a(h, u, 2).start()
 
     def gathered(u):
         for h in range(N):
             arrived(sib_r.at[h, u], ROWS, (hs2, ht2)[u])
 
-    def student():
+    def student(core, add):
         def tile(i):
-            at = pl.ds(pl.multiple_of(i * TILE, TILE), TILE)
-            rows = x[:, :, :, :, :hs].reshape(N * ROWS, hs)
-            logits = jnp.dot(rows, ws[:, at], preferred_element_type=jnp.float32)
-            logit_s[:, :, at] = logits.reshape(N, ROWS, TILE)
-
-        loop(0, vs // TILE, tile)
-
-    def teacher():
+            at = pl.ds(pl.multiple_of(i * (vs // 2), 128), vs // 2)
+            rows = x[:, :, :, :, span(0, core)].reshape(N * ROWS, hs2)
+            logits = jnp.dot(rows, ws[span(0, core), at], preferred_element_type=jnp.float32)
+            logits = logits.reshape(N, ROWS, vs // 2)
+            logit_s[:, :, at] = logit_s[:, :, at] + logits if add else logits
+
+        loop(0, 2, tile)
+
+    wt_span = lambda core: pl.ds(pl.multiple_of(core * ht2, 128), ht2)
+
+    def teacher_own():
         def tile(i):
-            at = pl.ds(pl.multiple_of(i * TILE, TILE), TILE)
-            rows = x[:, :, :, :, hs:].reshape(N * ROWS, ht)
-            logits = jnp.dot(rows, wt[:, at], preferred_element_type=jnp.float32)
-            logit_t[:, :, at] = logits.reshape(N, ROWS, TILE)
-
-        loop(0, vs // TILE, tile)
+            at = pl.ds(pl.multiple_of(i * (vs // 2), 128), vs // 2)
+            rows = x[:, :, :, :, span(1, c)].reshape(N * ROWS, ht2)
+            logits = jnp.dot(rows, wt[wt_span(c), at], preferred_element_type=jnp.float32)
+            logit_t[:, :, at] = logits.reshape(N, ROWS, vs // 2)
+
+        loop(0, 2, tile)
+
+    def teacher(h):
+        def tile(i):
+            at = pl.ds(pl.multiple_of(i * (vs // 2), 128), vs // 2)
+            rows = x[h, :, :, :, span(1, 1 - c)].reshape(ROWS, ht2)
+            logits = jnp.dot(rows, wt[wt_span(1 - c), at], preferred_element_type=jnp.float32)
+            logit_t[h, :, at] = logit_t[h, :, at] + logits
+
+        loop(0, 2, tile)
 
     lane = lax.broadcasted_iota(jnp.int32, (1, 128), 1)
 
@@ -253,8 +331,15 @@
             sum_t = sum_t + jnp.exp(b[3:4] - peak_t) * b[4:5]
         return peak_s, sum_s, cross, peak_t, sum_t
 
+    def to_sibling(src, dst, ssem, rsem):
+        return rcopy(src, dst, ssem, rsem, dev(0, 0, 1))
+
+    def stats_sib(h):
+        return to_sibling(stat_own.at[h], stat_sib.at[h], ss_s, ss_r.at[h])
+
     def stats_z(h):
         stat_own[h] = jnp.transpose(stat_col[h])[:8, :]
+        stats_sib(h).start()
         loop(1, NZ, lambda k: sz(h, k).start())
 
     def stats_y(h):
@@ -271,48 +356,65 @@
         lse_s, lse_t = peak_s + jnp.log(sum_s), peak_t + jnp.log(sum_t)
         kl = cross / sum_s - lse_s + lse_t
         offset = lse_s - lse_t + kl
-        scale = jnp.exp(stat_own[h][0:1] - lse_s)
-        local_mean = stat_own[h][5:6]
-        packed = jnp.concatenate(
-            [scale, offset - local_mean, kl, jnp.zeros((125, ROWS), jnp.float32)], axis=0
-        )
+        stats_sib(h).wait_recv()
+        both = []
+        for stat in (stat_own[h], stat_sib[h]):
+            both += [jnp.exp(stat[0:1] - lse_s), offset - stat[5:6]]
+        packed = jnp.concatenate(both + [kl, jnp.zeros((123, ROWS), jnp.float32)], axis=0)
         fac[h] = jnp.transpose(packed)
 
-    def grads(h):
+    def e_sib():
+        return to_sibling(e_rows, e_in, ge_s, ge_r)
+
+    def a_sib(h):
+        return to_sibling(a_rows.at[h], a_in.at[h], ga_s, ga_r.at[h])
+
+    def head_sib():
+        return to_sibling(ws.at[span(0, 1 - c)], w_in, w_s, w_r)
+
+    def grads_e():
+        for h in range(N):
+            def some(at):
+                e_rows[h, at, :] = exp_s[h, at, :].astype(jnp.bfloat16)
+
+            groups(some)
+        e_sib().start()
+
+    def grads_a(h):
         def some(at):
-            e = exp_s[h, at, :]
             ratio = logit_s[h, at, :] - logit_t[h, at, :]
-            gb_rows[at, :] = (e * (ratio - stat_col[h, at, 5:6])).astype(jnp.bfloat16)
-            gb_rows[pl.ds(ROWS + at.start, PART), :] = e.astype(jnp.bfloat16)
+            a = exp_s[h, at, :] * (ratio - stat_col[h, at, 5:6])
+            a_rows[h, at, :] = a.astype(jnp.bfloat16)
 
         groups(some)
+        a_sib(h).start()
 
     part = hs2 // 2
 
-    def transpose(lo, hi):
+    def transpose(n, src, start):
         def block(i):
             at = pl.ds(pl.multiple_of(i * TILE, TILE), TILE)
-            wst[:, at] = jnp.transpose(ws[at, :])
+            rows = pl.ds(pl.multiple_of(start + i * TILE, TILE), TILE)
+            wst[n, :, at] = jnp.transpose(src[rows, :])
+
+        loop(0, hs2 // TILE, block)
+
+    def back_e(n, lo, hi):
+        def block(i):
+            at = pl.ds(pl.multiple_of(i * part, 128), part)
+            rows = (e_rows, e_in)[n][...].reshape(N * ROWS, vs)
+            sums = jnp.dot(rows, wst[n, :, at], preferred_element_type=jnp.float32)
+            sum_e[n, :, :, at] = sums.reshape(N, ROWS, part)
 
         loop(lo, hi, block)
 
-    def back(h, lo, hi):
+    def back_a(h, n):
         def block(i):
-            at = pl.ds(pl.multiple_of(i * 2 * TILE, 2 * TILE), 2 * TILE)
-            ab[h, :, at] = jnp.dot(
-                gb_rows[...], wst[:, at], preferred_element_type=jnp.float32
-            )
-
-        loop(lo, hi, block)
-
-    def mixed(h, core, i):
-        w = wcol[:, :, h, :, 0:1].reshape(ROWS, 1)
-        at = pl.ds(pl.multiple_of(core * hs2 + i * part, 128), part)
-        scale, offset = fac[h, :, 0:1] * w, fac[h, :, 1:2]
-        return scale * (ab[h, :ROWS, at] - offset * ab[h, ROWS:, at])
-
-    def swap(h, i):
-        return rcopy(ps.at[h, i], pr.at[h, i], ps_s, ps_r.at[h, i], dev(0, 0, 1))
+            at = pl.ds(pl.multiple_of(i * part, 128), part)
+            rows = (a_rows, a_in)[n][h]
+            sum_a[n, h, :, at] = jnp.dot(rows, wst[n, :, at], preferred_element_type=jnp.float32)
+
+        loop(0, 2, block)
 
     def ra1(h, j):
         return rcopy(
@@ -338,19 +440,16 @@
             rb2_s, rb2_r, dev(j, 0, 0),
         )
 
-    def mix(h):
+    def reduce_first(h):
+        w = wcol[:, :, h, :, 0:1].reshape(ROWS, 1)
+        f = [fac[h, :, n:n + 1] for n in range(4)]
         for i in range(2):
-            ps[h, i] = mixed(h, 1 - c, i)
-            swap(h, i).start()
-
-    def reduce_first(h):
-        for i in range(2):
-            total = mixed(h, c, i)
-            swap(h, i).wait_recv()
-            total = total + pr[h, i]
-            r1[h, :, :, :, i * part:(i + 1) * part] = (
-                total.astype(jnp.bfloat16).reshape(NY, HZ, BLK, part)
-            )
+            at = slice(i * part, (i + 1) * part)
+            total = 0.0
+            for n in range(2):
+                some = sum_a[n, h, :, at] - f[2 * n + 1] * sum_e[n, h, :, at]
+                total = total + (f[2 * n] * w) * some
+            r1[h, :, :, :, at] = total.astype(jnp.bfloat16).reshape(NY, HZ, BLK, part)
         loop(1, NY, lambda j: ra1(h, j).start())
         ahead(h, lambda k: rb1(h, k).start())
 
@@ -393,7 +492,7 @@
             theirs = pl.ds(pl.multiple_of((1 - c) * hs2, 128), hs2)
             out_ref[:, mine] = fin[pl.ds(pl.multiple_of(c * 8, 8), 8), :]
             at = pl.multiple_of((y * HZ + zz) * BLK + c * 8, 8)
-            kl = fac[h, pl.ds(at, 8), 2:3]
+            kl = fac[h, pl.ds(at, 8), 4:5]
             row = lax.broadcasted_iota(jnp.int32, (8, 128), 0)
             col = lax.broadcasted_iota(jnp.int32, (8, 128), 1)
             kl = jnp.sum(jnp.where(row == col, kl, 0.0), axis=0, keepdims=True)
@@ -412,45 +511,75 @@
     def rest_left():
         arrived_f32(sz_s, stat_z.at[:, pl.ds(1, NZ - 1)])
         arrived_f32(sy_s, stat_y.at[:, pl.ds(1, NY * NC - 1)])
-        arrived_f32(ps_s, ps)
+        head_sib().wait_send()
+        arrived_f32(ss_s, stat_sib)
+        arrived_f32(ge_s, e_rows)
+        arrived_f32(ga_s, a_rows)
         arrived(ra1_s, N * (NY - 1) * HZ * BLK, ga)
         arrived(rb1_s, (NZ - 1) * NY * BLK, gb)
         arrived(ra2_s, (NZ - 1) * BLK, ga)
         arrived(rb2_s, (NY - 1) * BLK, gb)
 
     for u in range(2):
-        for h in range(N):
-            send_first(h, u)
+        send_first(u)
     load_s.wait()
-    transpose(0, hs // TILE)
-    for u in range(2):
-        for h in range(N):
-            relay(h, u)
+    head_sib().start()
+    transpose(0, ws, c * hs2)
+    relay_b(0)
+    relay(0, 0)
+    relay_b(1)
+    relay(1, 0)
+    relay(0, 1)
+    relay_b2(0)
+    send_sibling_own(0)
+    relay_y(0, 0)
+    relay(1, 1)
+    relay_y(0, 1)
+    relay_b2(1)
+    send_sibling_own(1)
+    relay_y(1, 0)
+    head_sib().wait_recv()
+    transpose(1, w_in, 0)
+    relay_y(1, 1)
     load_t.wait()
     for h in range(N):
-        send_sibling(h, 0)
+        send_sibling_a(h, 0)
+    send_sibling_b(0)
+    for h in range(N):
+        send_sibling_last(h, 0)
+    student(c, False)
     gathered(0)
-    student()
+    student(1 - c, True)
+    for h in range(N):
+        send_sibling_a(h, 1)
+    send_sibling_b(1)
     for h in range(N):
         stats_s(h)
     for h in range(N):
-        send_sibling(h, 1)
+        send_sibling_last(h, 1)
+    teacher_own()
+    grads_e()
     gathered(1)
-    teacher()
-    for h in range(N):
+    for h in range(N):
+        teacher(h)
         stats_t(h)
         stats_z(h)
-    grads(0)
-    back(0, 0, 5)
+    for h in range(N):
+        grads_a(h)
+    back_e(0, 0, 2)
     stats_y(0)
+    back_a(0, 0)
     stats_y(1)
-    grads(1)
-    back(1, 0, 5)
+    e_sib().wait_recv()
+    back_e(1, 0, 2)
+    a_sib(0).wait_recv()
+    back_a(0, 1)
     factors(0)
-    mix(0)
+    reduce_first(0)
+    back_a(1, 0)
+    a_sib(1).wait_recv()
+    back_a(1, 1)
     factors(1)
-    mix(1)
-    reduce_first(0)
     reduce_first(1)
     reduce_second(0)
     gather_left()
@@ -485,7 +614,8 @@
         out_specs=vmem,
         scratch_shapes=[
             pltpu.VMEM((hs, vs), bf16),
-            pltpu.VMEM((vs, hs), bf16),
+            pltpu.VMEM((hs2, vs), bf16),
+            pltpu.VMEM((2, vs, hs2), bf16),
             pltpu.VMEM((ht, vs), bf16),
             pltpu.VMEM((N, NY, HZ, BLK, hs + ht), bf16),
             pltpu.VMEM((rows, (hs + ht) // 2), f32),
@@ -493,17 +623,20 @@
             pltpu.VMEM((N, ROWS, vs), f32),
             pltpu.VMEM((N, ROWS, vs), f32),
             pltpu.VMEM((N, ROWS, vs), f32),
-            pltpu.VMEM((N, 2 * ROWS, hs), f32),
+            pltpu.VMEM((2, N, ROWS, hs2), f32),
+            pltpu.VMEM((2, N, ROWS, hs2), f32),
             pltpu.VMEM((N, ROWS, 128), f32),
+            pltpu.VMEM((N, 8, ROWS), f32),
             pltpu.VMEM((N, 8, ROWS), f32),
             pltpu.VMEM((N, NZ, 8, ROWS), f32),
             pltpu.VMEM((N, 8, ROWS), f32),
             pltpu.VMEM((N, NY * NC, 8, ROWS), f32),
             pltpu.VMEM((N, ROWS, 128), f32),
             pltpu.VMEM((NY, HZ, N, BLK, 128), f32),
-            pltpu.VMEM((2 * ROWS, vs), bf16),
-            pltpu.VMEM((N, 2, ROWS, hs2 // 2), f32),
-            pltpu.VMEM((N, 2, ROWS, hs2 // 2), f32),
+            pltpu.VMEM((N, ROWS, vs), bf16),
+            pltpu.VMEM((N, ROWS, vs), bf16),
+            pltpu.VMEM((N, ROWS, vs), bf16),
+            pltpu.VMEM((N, ROWS, vs), bf16),
             pltpu.VMEM((N, NY, HZ, BLK, hs2), bf16),
             pltpu.VMEM((N, NY, HZ, BLK, ga), bf16),
             pltpu.VMEM((N, HZ, BLK, ga), bf16),
@@ -514,16 +647,17 @@
             pltpu.VMEM((BLK, hs2), f32),
             pltpu.VMEM((8, hs2), f32),
             dma((2,)), dma(()), dma(()),
-            dma((2,)), dma((N, 2, HZ)), dma((2,)), dma((N, 2)),
-            dma((2,)), dma((2,)), dma((2,)), dma((N, 2)),
+            dma((2,)), dma((N, 2, HZ)), dma((2,)), dma((N, 2)), dma((N, 2)), dma((N, 2)),
+            dma((2,)), dma((2,)), dma((2,)), dma((2,)), dma((2, 2)),
             dma((2,)), dma((N, 2)),
-            dma(()), dma((N,)), dma(()), dma((N,)), dma(()), dma((N, 2)),
+            dma(()), dma((N,)), dma(()), dma((N,)), dma(()), dma(()), dma(()), dma((N,)),
+            dma(()), dma(()), dma(()), dma((N,)),
             dma(()), dma((N,)), dma(()), dma(()),
             dma(()), dma(()), dma(()), dma(()),
             dma(()), dma(()),
         ],
         compiler_params=pltpu.CompilerParams(
-            collective_id=0, has_side_effects=True, vmem_limit_bytes=56 * 1024 * 1024
+            collective_id=0, has_side_effects=True, vmem_limit_bytes=60 * 1024 * 1024
         ),
         cost_estimate=pl.CostEstimate(
             flops=flops, bytes_accessed=2 * vs * (hs + ht), transcendentals=2 * tokens * vs

time: 79.8 us -> 72.1 us (0.904)
  Pallas kernels: 79 us -> 71.3 us
    pallas_call x1, Pallas kernels: 77.4 us -> 69.8 us  [local(): pl.pallas_call(functools.partial(kernel, hs, ht, vs), out_shape=jax.Shape...]
where the time goes in v3:
time: 72.1 us; the launch traced here: 71.9 us
  Pallas kernels  71.3 us (99%)
    pallas_call x1, Pallas kernels, local(): pl.pallas_call(functools.partial(kernel, hs, ht, vs), out_shape=jax.Shape...  69.8 us
    pallas_call x1, Pallas kernels, local(): pl.pallas_call(split, out_shape=(jax.ShapeDtypeStruct((1, rows), f32), ja...  1.51 us

profile of v3, /device:TPU:37, one launch (start us, length us, event | category | flops | bytes accessed | tf_op | source)
XLA Modules:
  0.0 71.9 jit_solution(15894017061491380407)
XLA Ops:
  0.6 69.8 %shard_map.77.result_ref = f32[8,2688]{1,0:T(8,128)} custom-call(bf16[8,2560]{1,0:T(8,128)(2,1)} %sh_ref.1, bf16[8,2048]{1,0:T(8,128)(2,1)} %th_ref.1, s32[1,512]{1,0:T(1,128)} %bitcast.3, s32[1,512]{1,0:T(1,128)} %bitcast.4, bf16[2560,1280]{1,0:T(8,128)(2,1)} %ws_hbm.1, bf16[2048,1280]{1,0:T(8,128)(2,1)} %wt_hbm.1), custom_call_target="tpu_custom_call" | custom-call | flops 9395240960 | bytes 11796480 | tf_op jit(solution)/shard_map/pallas_call | solution.py:610
  70.4 1.5 %shard_map.78 = (f32[1,8]{1,0:T(1,128)}, bf16[8,2560]{1,0:T(8,128)(2,1)}) custom-call(f32[8,2688]{1,0:T(8,128)} %shard_map.77.result_ref), custom_call_target="tpu_custom_call" | custom-call | tf_op jit(solution)/shard_map/pallas_call | solution.py:670

commit v4 on v3

--- a/solution.py
+++ b/solution.py
@@ -15,8 +15,12 @@
 ROWS = NY * HZ * BLK
 TILE = 256
 GROUP, PART = 128, 32
-SPLIT_S, SPLIT_T, SPLIT_G = 1024, 768, 896
+SPLIT_S, SPLIT_T, SPLIT_G = 1024, 640, 896
 MESH = pl.DeviceIdType.MESH
+
+
+def wide_half(width):
+    return (width + 255) // 256 * 128
 
 
 def kernel(
@@ -25,11 +29,11 @@
     out_ref,
     ws, w_in, wst, wt, x, xf, xg, logit_s, logit_t, exp_s,
     sum_e, sum_a, stat_col, stat_own, stat_sib, stat_z, stat_mid, stat_y, fac, wcol,
-    e_rows, e_in, a_rows, a_in, r1, ra, r2a, ra2, rb, r2b, rb2, fin, fin_in,
+    e_rows, e_in, a_rows, a_in, r1, ra, r2a, ra2, rb, r2b, rb2,
     load_sem, pair_s, pair_r,
     a1_s, a1_r, a2_s, a2_r, a2f_r, a3_r, b1_s, b1_r, b2_s, b2_r, b2f_r, sib_s, sib_r,
     sz_s, sz_r, sy_s, sy_r, w_s, w_r, ss_s, ss_r, ge_s, ge_r, ga_s, ga_r,
-    ra1_s, ra1_r, ra2_s, ra2_r, rb1_s, rb1_r, rb2_s, rb2_r, fin_s, fin_r,
+    ra1_s, ra1_r, ra2_s, ra2_r, rb1_s, rb1_r, rb2_s, rb2_r,
 ):
     v = lax.axis_index("vocab")
     y, z, c = v // (NZ * NC), (v // NC) % NZ, v % NC
@@ -38,6 +42,7 @@
     sa, ta = SPLIT_S, SPLIT_T
     ga = SPLIT_G
     gb = hs2 - ga
+    ha, hb = wide_half(ga), wide_half(gb)
     widths = ((sa, hs2 - sa), (ta, ht2 - ta))
 
     def dev(dy, dz, dc):
@@ -56,6 +61,7 @@
 
     barrier = pltpu.get_barrier_semaphore()
     partners = [(0, k, 0) for k in range(1, NZ)]
+    partners += [(0, k, 1) for k in range(1, NZ)]
     partners += [(j, 0, d) for j in range(1, NY) for d in range(NC)] + [(0, 0, 1)]
     for p in partners:
         pl.semaphore_signal(barrier, inc=1, device_id=dev(*p), device_id_type=MESH)
@@ -251,33 +257,18 @@
 
     def student(core, add):
         def tile(i):
-            at = pl.ds(pl.multiple_of(i * (vs // 2), 128), vs // 2)
+            at = pl.ds(pl.multiple_of(i * vs, 128), vs)
             rows = x[:, :, :, :, span(0, core)].reshape(N * ROWS, hs2)
             logits = jnp.dot(rows, ws[span(0, core), at], preferred_element_type=jnp.float32)
-            logits = logits.reshape(N, ROWS, vs // 2)
+            logits = logits.reshape(N, ROWS, vs)
             logit_s[:, :, at] = logit_s[:, :, at] + logits if add else logits
 
-        loop(0, 2, tile)
-
-    wt_span = lambda core: pl.ds(pl.multiple_of(core * ht2, 128), ht2)
-
-    def teacher_own():
-        def tile(i):
-            at = pl.ds(pl.multiple_of(i * (vs // 2), 128), vs // 2)
-            rows = x[:, :, :, :, span(1, c)].reshape(N * ROWS, ht2)
-            logits = jnp.dot(rows, wt[wt_span(c), at], preferred_element_type=jnp.float32)
-            logit_t[:, :, at] = logits.reshape(N, ROWS, vs // 2)
-
-        loop(0, 2, tile)
-
-    def teacher(h):
-        def tile(i):
-            at = pl.ds(pl.multiple_of(i * (vs // 2), 128), vs // 2)
-            rows = x[h, :, :, :, span(1, 1 - c)].reshape(ROWS, ht2)
-            logits = jnp.dot(rows, wt[wt_span(1 - c), at], preferred_element_type=jnp.float32)
-            logit_t[h, :, at] = logit_t[h, :, at] + logits
-
-        loop(0, 2, tile)
+        tile(0)
+
+    def teacher():
+        rows = x[:, :, :, :, hs:].reshape(N * ROWS, ht)
+        logits = jnp.dot(rows, wt[...], preferred_element_type=jnp.float32)
+        logit_t[...] = logits.reshape(N, ROWS, vs)
 
     lane = lax.broadcasted_iota(jnp.int32, (1, 128), 1)
 
@@ -399,22 +390,17 @@
 
         loop(0, hs2 // TILE, block)
 
-    def back_e(n, lo, hi):
-        def block(i):
-            at = pl.ds(pl.multiple_of(i * part, 128), part)
-            rows = (e_rows, e_in)[n][...].reshape(N * ROWS, vs)
-            sums = jnp.dot(rows, wst[n, :, at], preferred_element_type=jnp.float32)
-            sum_e[n, :, :, at] = sums.reshape(N, ROWS, part)
-
-        loop(lo, hi, block)
+    def back_e(h, n):
+        rows = (e_rows, e_in)[n][h]
+        sum_e[n, h] = jnp.dot(rows, wst[n], preferred_element_type=jnp.float32)
 
     def back_a(h, n):
         def block(i):
-            at = pl.ds(pl.multiple_of(i * part, 128), part)
+            at = pl.ds(pl.multiple_of(i * hs2, 128), hs2)
             rows = (a_rows, a_in)[n][h]
             sum_a[n, h, :, at] = jnp.dot(rows, wst[n, :, at], preferred_element_type=jnp.float32)
 
-        loop(0, 2, block)
+        block(0)
 
     def ra1(h, j):
         return rcopy(
@@ -428,17 +414,29 @@
             rb1_s, rb1_r, dev(0, k, 0),
         )
 
-    def rra2(h, k):
+    def rra2(h, k, d):
         return rcopy(
-            r2a.at[h, ((z + k) % NZ) // N], ra2.at[h, k],
-            ra2_s, ra2_r, dev(0, k, 0),
-        )
-
-    def rrb2(h, j):
+            r2a.at[h, (c + d) % NC, ((z + k) % NZ) // N], ra2.at[d, k],
+            ra2_s, ra2_r, dev(0, k, d),
+        )
+
+    def rrb2(h, j, d):
         return rcopy(
-            r2b.at[h, (y + j) % NY], rb2.at[h, j],
-            rb2_s, rb2_r, dev(j, 0, 0),
-        )
+            r2b.at[(c + d) % NC, (y + j) % NY], rb2.at[d, j],
+            rb2_s, rb2_r, dev(j, 0, d),
+        )
+
+    def by_core(total):
+        width = total.shape[-1]
+        half = wide_half(width)
+        fill = jnp.zeros(total.shape[:1] + (8, 2 * half - width), jnp.float32)
+        packed = []
+        for rows in (total[:, :8], total[:, 8:]):
+            right = rows[..., half:]
+            if 2 * half > width:
+                right = jnp.concatenate([right, fill], axis=2)
+            packed.append(jnp.concatenate([rows[..., :half], right], axis=1).astype(jnp.bfloat16))
+        return packed
 
     def reduce_first(h):
         w = wcol[:, :, h, :, 0:1].reshape(ROWS, 1)
@@ -458,8 +456,14 @@
         total = r1[h, y, :, :, :ga].astype(jnp.float32)
         for j in range(1, NY):
             total = total + ra[h, j].astype(jnp.float32)
-        r2a[h] = total.astype(jnp.bfloat16)
-        ahead(h, lambda k: rra2(h, k).start())
+        for d, rows in enumerate(by_core(total)):
+            r2a[h, d] = rows
+
+        def give(k):
+            rra2(h, k, 0).start()
+            rra2(h, k, 1).start()
+
+        ahead(h, give)
 
         @pl.when(own == h)
         def _():
@@ -467,38 +471,36 @@
             total = r1[h, :, zz, :, ga:].astype(jnp.float32)
             for k in range(1, NZ):
                 total = total + rb[h, k].astype(jnp.float32)
-            r2b[h] = total.astype(jnp.bfloat16)
-            loop(1, NY, lambda j: rrb2(h, j).start())
+            for d, rows in enumerate(by_core(total)):
+                r2b[d] = rows
+            rra2(h, 0, 1).start()
+            loop(1, 2 * NY, lambda n: rrb2(h, n // 2, n % 2).start())
 
     def final(h):
         @pl.when(own == h)
         def _():
-            arrived(ra2_r, (NZ - 1) * BLK, ga)
-            arrived(rb2_r, (NY - 1) * BLK, gb)
-            left = r2a[h, zz].astype(jnp.float32)
-            for k in range(1, NZ):
-                left = left + ra2[h, k].astype(jnp.float32)
-            right = r2b[h, y].astype(jnp.float32)
-            for j in range(1, NY):
-                right = right + rb2[h, j].astype(jnp.float32)
-            fin[:, :ga] = left
-            fin[:, ga:] = right
-            give = rcopy(
-                fin.at[pl.ds(pl.multiple_of((1 - c) * 8, 8), 8), :], fin_in,
-                fin_s, fin_r, dev(0, 0, 1),
-            )
-            give.start()
-            mine = pl.ds(pl.multiple_of(c * hs2, 128), hs2)
-            theirs = pl.ds(pl.multiple_of((1 - c) * hs2, 128), hs2)
-            out_ref[:, mine] = fin[pl.ds(pl.multiple_of(c * 8, 8), 8), :]
+            arrived(ra2_r, (2 * NZ - 1) * BLK, ha)
+            arrived(rb2_r, (2 * NY - 1) * BLK, hb)
+            for d in range(NC):
+                left = (ra2[d, 0] if d else r2a[h, c, zz]).astype(jnp.float32)
+                for k in range(1, NZ):
+                    left = left + ra2[d, k].astype(jnp.float32)
+                right = (rb2[d, 0] if d else r2b[c, y]).astype(jnp.float32)
+                for j in range(1, NY):
+                    right = right + rb2[d, j].astype(jnp.float32)
+                start = 0
+                for some, width in ((left, ga), (right, gb)):
+                    half = some.shape[-1]
+                    for rows, some_width in ((some[:8], half), (some[8:], width - half)):
+                        at = pl.multiple_of(((c + d) % NC) * hs2 + start, 128)
+                        out_ref[:, pl.ds(at, some_width)] = rows[:, :some_width]
+                        start += some_width
             at = pl.multiple_of((y * HZ + zz) * BLK + c * 8, 8)
             kl = fac[h, pl.ds(at, 8), 4:5]
             row = lax.broadcasted_iota(jnp.int32, (8, 128), 0)
             col = lax.broadcasted_iota(jnp.int32, (8, 128), 1)
             kl = jnp.sum(jnp.where(row == col, kl, 0.0), axis=0, keepdims=True)
             out_ref[:, hs:] = jnp.broadcast_to(kl, (8, 128))
-            give.wait()
-            out_ref[:, theirs] = fin_in[...]
 
     def gather_left():
         for u in range(2):
@@ -517,14 +519,14 @@
         arrived_f32(ga_s, a_rows)
         arrived(ra1_s, N * (NY - 1) * HZ * BLK, ga)
         arrived(rb1_s, (NZ - 1) * NY * BLK, gb)
-        arrived(ra2_s, (NZ - 1) * BLK, ga)
-        arrived(rb2_s, (NY - 1) * BLK, gb)
-
-    for u in range(2):
-        send_first(u)
+        arrived(ra2_s, (2 * NZ - 1) * BLK, ha)
+        arrived(rb2_s, (2 * NY - 1) * BLK, hb)
+
+    send_first(0)
     load_s.wait()
     head_sib().start()
     transpose(0, ws, c * hs2)
+    send_first(1)
     relay_b(0)
     relay(0, 0)
     relay_b(1)
@@ -557,25 +559,26 @@
         stats_s(h)
     for h in range(N):
         send_sibling_last(h, 1)
-    teacher_own()
     grads_e()
     gathered(1)
-    for h in range(N):
-        teacher(h)
+    teacher()
+    for h in range(N):
         stats_t(h)
         stats_z(h)
     for h in range(N):
         grads_a(h)
-    back_e(0, 0, 2)
+    back_e(0, 0)
+    back_a(0, 0)
     stats_y(0)
-    back_a(0, 0)
+    e_sib().wait_recv()
+    back_e(0, 1)
     stats_y(1)
-    e_sib().wait_recv()
-    back_e(1, 0, 2)
     a_sib(0).wait_recv()
     back_a(0, 1)
+    back_e(1, 0)
     factors(0)
     reduce_first(0)
+    back_e(1, 1)
     back_a(1, 0)
     a_sib(1).wait_recv()
     back_a(1, 1)
@@ -602,6 +605,7 @@
     tokens = segment_ids.shape[0]
     hs2 = hs // 2
     ga, gb = SPLIT_G, hs2 - SPLIT_G
+    ha, hb = wide_half(ga), wide_half(gb)
     f32, bf16 = jnp.float32, jnp.bfloat16
     dma = pltpu.SemaphoreType.DMA
     vmem = pl.BlockSpec(memory_space=pltpu.VMEM)
@@ -639,13 +643,11 @@
             pltpu.VMEM((N, ROWS, vs), bf16),
             pltpu.VMEM((N, NY, HZ, BLK, hs2), bf16),
             pltpu.VMEM((N, NY, HZ, BLK, ga), bf16),
-            pltpu.VMEM((N, HZ, BLK, ga), bf16),
-            pltpu.VMEM((N, NZ, BLK, ga), bf16),
+            pltpu.VMEM((N, NC, HZ, BLK, ha), bf16),
+            pltpu.VMEM((NC, NZ, BLK, ha), bf16),
             pltpu.VMEM((N, NZ, NY, BLK, gb), bf16),
-            pltpu.VMEM((N, NY, BLK, gb), bf16),
-            pltpu.VMEM((N, NY, BLK, gb), bf16),
-            pltpu.VMEM((BLK, hs2), f32),
-            pltpu.VMEM((8, hs2), f32),
+            pltpu.VMEM((NC, NY, BLK, hb), bf16),
+            pltpu.VMEM((NC, NY, BLK, hb), bf16),
             dma((2,)), dma(()), dma(()),
             dma((2,)), dma((N, 2, HZ)), dma((2,)), dma((N, 2)), dma((N, 2)), dma((N, 2)),
             dma((2,)), dma((2,)), dma((2,)), dma((2,)), dma((2, 2)),
@@ -654,7 +656,6 @@
             dma(()), dma(()), dma(()), dma((N,)),
             dma(()), dma((N,)), dma(()), dma(()),
             dma(()), dma(()), dma(()), dma(()),
-            dma(()), dma(()),
         ],
         compiler_params=pltpu.CompilerParams(
             collective_id=0, has_side_effects=True, vmem_limit_bytes=60 * 1024 * 1024

time: 72.1 us -> 70.9 us (0.983)
  Pallas kernels: 71.3 us -> 70 us
    pallas_call x1, Pallas kernels: 69.8 us -> 68.5 us  [local(): pl.pallas_call(functools.partial(kernel, hs, ht, vs), out_shape=jax.Shape...]
where the time goes in v4:
time: 70.9 us; the launch traced here: 70.7 us
  Pallas kernels  70 us (99%)
    pallas_call x1, Pallas kernels, local(): pl.pallas_call(functools.partial(kernel, hs, ht, vs), out_shape=jax.Shape...  68.5 us
    pallas_call x1, Pallas kernels, local(): pl.pallas_call(split, out_shape=(jax.ShapeDtypeStruct((1, rows), f32), ja...  1.51 us

profile of v4, /device:TPU:37, one launch (start us, length us, event | category | flops | bytes accessed | tf_op | source)
XLA Modules:
  0.0 70.7 jit_solution(6300515777072740953)
XLA Ops:
  0.6 68.5 %shard_map.77.result_ref = f32[8,2688]{1,0:T(8,128)} custom-call(bf16[8,2560]{1,0:T(8,128)(2,1)} %sh_ref.1, bf16[8,2048]{1,0:T(8,128)(2,1)} %th_ref.1, s32[1,512]{1,0:T(1,128)} %bitcast.3, s32[1,512]{1,0:T(1,128)} %bitcast.4, bf16[2560,1280]{1,0:T(8,128)(2,1)} %ws_hbm.1, bf16[2048,1280]{1,0:T(8,128)(2,1)} %wt_hbm.1), custom_call_target="tpu_custom_call" | custom-call | flops 9395240960 | bytes 11796480 | tf_op jit(solution)/shard_map/pallas_call | solution.py:614
  69.2 1.5 %shard_map.78 = (f32[1,8]{1,0:T(1,128)}, bf16[8,2560]{1,0:T(8,128)(2,1)}) custom-call(f32[8,2688]{1,0:T(8,128)} %shard_map.77.result_ref), custom_call_target="tpu_custom_call" | custom-call | tf_op jit(solution)/shard_map/pallas_call | solution.py:671

commit v5 on v4

--- a/solution.py
+++ b/solution.py
@@ -285,6 +285,7 @@
             peak = jnp.max(s, axis=1, keepdims=True)
             e = jnp.exp(s - peak)
             exp_s[h, at, :] = e
+            e_rows[h, at, :] = e.astype(jnp.bfloat16)
             total = jnp.sum(e, axis=1, keepdims=True)
             stat_col[h, at, :] = jnp.where(lane == 0, peak, jnp.where(lane == 1, total, 0.0))
 
@@ -363,14 +364,6 @@
     def head_sib():
         return to_sibling(ws.at[span(0, 1 - c)], w_in, w_s, w_r)
 
-    def grads_e():
-        for h in range(N):
-            def some(at):
-                e_rows[h, at, :] = exp_s[h, at, :].astype(jnp.bfloat16)
-
-            groups(some)
-        e_sib().start()
-
     def grads_a(h):
         def some(at):
             ratio = logit_s[h, at, :] - logit_t[h, at, :]
@@ -402,9 +395,10 @@
 
         block(0)
 
-    def ra1(h, j):
+    def ra1(h, j, start, width):
+        at = pl.ds(start, width)
         return rcopy(
-            r1.at[h, (y + j) % NY, :, :, pl.ds(0, ga)], ra.at[h, j],
+            r1.at[h, (y + j) % NY, :, :, at], ra.at[h, j, :, :, at],
             ra1_s, ra1_r.at[h], dev(j, 0, 0),
         )
 
@@ -448,7 +442,8 @@
                 some = sum_a[n, h, :, at] - f[2 * n + 1] * sum_e[n, h, :, at]
                 total = total + (f[2 * n] * w) * some
             r1[h, :, :, :, at] = total.astype(jnp.bfloat16).reshape(NY, HZ, BLK, part)
-        loop(1, NY, lambda j: ra1(h, j).start())
+            start, width = (0, part) if i == 0 else (part, ga - part)
+            loop(1, NY, lambda j, start=start, width=width: ra1(h, j, start, width).start())
         ahead(h, lambda k: rb1(h, k).start())
 
     def reduce_second(h):
@@ -559,7 +554,7 @@
         stats_s(h)
     for h in range(N):
         send_sibling_last(h, 1)
-    grads_e()
+    e_sib().start()
     gathered(1)
     teacher()
     for h in range(N):

time: 70.9 us -> 70.8 us (level)
  no operation moved by 1% of the time
where the time goes in v5:
time: 70.8 us; the launch traced here: 70.6 us
  Pallas kernels  70 us (99%)
    pallas_call x1, Pallas kernels, local(): pl.pallas_call(functools.partial(kernel, hs, ht, vs), out_shape=jax.Shape...  68.5 us
    pallas_call x1, Pallas kernels, local(): pl.pallas_call(split, out_shape=(jax.ShapeDtypeStruct((1, rows), f32), ja...  1.51 us

profile of v5, /device:TPU:37, one launch (start us, length us, event | category | flops | bytes accessed | tf_op | source)
XLA Modules:
  0.0 70.6 jit_solution(10325232467328083674)
XLA Ops:
  0.6 68.5 %shard_map.77.result_ref = f32[8,2688]{1,0:T(8,128)} custom-call(bf16[8,2560]{1,0:T(8,128)(2,1)} %sh_ref.1, bf16[8,2048]{1,0:T(8,128)(2,1)} %th_ref.1, s32[1,512]{1,0:T(1,128)} %bitcast.3, s32[1,512]{1,0:T(1,128)} %bitcast.4, bf16[2560,1280]{1,0:T(8,128)(2,1)} %ws_hbm.1, bf16[2048,1280]{1,0:T(8,128)(2,1)} %wt_hbm.1), custom_call_target="tpu_custom_call" | custom-call | flops 9395240960 | bytes 11796480 | tf_op jit(solution)/shard_map/pallas_call | solution.py:609
  69.1 1.5 %shard_map.78 = (f32[1,8]{1,0:T(1,128)}, bf16[8,2560]{1,0:T(8,128)(2,1)}) custom-call(f32[8,2688]{1,0:T(8,128)} %shard_map.77.result_ref), custom_call_target="tpu_custom_call" | custom-call | tf_op jit(solution)/shard_map/pallas_call | solution.py:666
